TPU v7x, 32 devices: a whole 2x2x4 slice. The times are simulated.
32 devices in a mesh: seq: 4 (over z), heads: 4 (over y, core), hid: 2 (over x).
Axes of the slice: x: 2, y: 2, z: 4, core: 2. Of those that a mesh axis runs over, the one named last changes fastest.
Arguments:
- tokens_in: bfloat16 [8, 2048, 1024], P(('seq', 'hid'), 'heads'), may hold values from -6 to 6
- first_value: bfloat16 [8, 2048, 1024], P(('seq', 'hid'), None, 'heads')
- cotangent: bfloat16 [8, 2048, 1024], P(('seq', 'hid'), 'heads')
- counts: int32 [8, 4], P(('seq', 'hid')), may hold values from 256 to 512, as said below
- segments: int32 [8, 2048], P(('seq', 'hid')), may hold values from 0 to 2, as said below
- positions: int32 [8, 2048], P(('seq', 'hid')), may hold values from 0 to 2047, as said below
- norm_gains: float32 [2, 1024], replicated
- gain_mean: float32 [2, 1024], replicated
- gain_var: float32 [2, 1024], replicated
- heads_in: float32 [3, 1024, 1024], P(None, ('seq', 'hid'), 'heads')
- heads_in_mean: float32 [3, 1024, 1024], P(None, ('seq', 'hid'), 'heads')
- heads_in_var: float32 [3, 1024, 1024], P(None, ('seq', 'hid'), 'heads')
- heads_out: float32 [1024, 1024], P('heads', ('seq', 'hid'))
- heads_out_mean: float32 [1024, 1024], P('heads', ('seq', 'hid'))
- heads_out_var: float32 [1024, 1024], P('heads', ('seq', 'hid'))
- gate_up: float32 [2, 1024, 2816], P(None, ('seq', 'heads'), 'hid')
- gate_up_mean: float32 [2, 1024, 2816], P(None, ('seq', 'heads'), 'hid')
- gate_up_var: float32 [2, 1024, 2816], P(None, ('seq', 'heads'), 'hid')
- down_proj: float32 [2816, 1024], P('hid', ('seq', 'heads'))
- down_mean: float32 [2816, 1024], P('hid', ('seq', 'heads'))
- down_var: float32 [2816, 1024], P('hid', ('seq', 'heads'))
Outputs:
- block_out: bfloat16 [8, 2048, 1024], P(('seq', 'hid'), 'heads')
- input_grad: float32 [8, 2048, 1024], P(('seq', 'hid'), 'heads')
- first_grad: float32 [8, 2048, 1024], P(('seq', 'hid'), None, 'heads')
- gains_new: float32 [2, 1024], replicated
- gain_mean_new: float32 [2, 1024], replicated
- gain_var_new: float32 [2, 1024], replicated
- heads_in_new: float32 [3, 1024, 1024], P(None, ('seq', 'hid'), 'heads')
- heads_in_mean_new: float32 [3, 1024, 1024], P(None, ('seq', 'hid'), 'heads')
- heads_in_var_new: float32 [3, 1024, 1024], P(None, ('seq', 'hid'), 'heads')
- heads_out_new: float32 [1024, 1024], P('heads', ('seq', 'hid'))
- heads_out_mean_new: float32 [1024, 1024], P('heads', ('seq', 'hid'))
- heads_out_var_new: float32 [1024, 1024], P('heads', ('seq', 'hid'))
- gate_up_new: float32 [2, 1024, 2816], P(None, ('seq', 'heads'), 'hid')
- gate_up_mean_new: float32 [2, 1024, 2816], P(None, ('seq', 'heads'), 'hid')
- gate_up_var_new: float32 [2, 1024, 2816], P(None, ('seq', 'heads'), 'hid')
- down_new: float32 [2816, 1024], P('hid', ('seq', 'heads'))
- down_mean_new: float32 [2816, 1024], P('hid', ('seq', 'heads'))
- down_var_new: float32 [2816, 1024], P('hid', ('seq', 'heads'))
- norms: float32 [14], replicated
- value_norms: float32 [2], replicated
Inputs may be any that keep to these rules, and one draw needn't show every extreme that they name: `counts`: in each group one shard holds exactly 512 used positions and another exactly 256. `segments`: never falling within a group. Sequence 1 starts within the used positions of the group's first shard and ends within those of its last; sequences 0 and 2 lie in the first and the last shard. `positions`: within a sequence, rising by one from position to position. In each group sequence 0 starts at 0 and sequence 1 ends at 2047.
All inputs are finite; a program needn't handle non-finite values.
Results may differ from a plain program's by a relative error of at most 0.034.
The roundings to bfloat16 on the way count: a program that leaves them out, or rounds other values in their place, can miss the bound.
Values may be sent and summed in bfloat16 or wider, within the bound.
No kernel may reach another device: no remote copies, remote signals or barrier semaphores. Data moves between devices by JAX's collectives and lax.ppermute only.
A program may use at most 320 MiB of HBM per device.

v0:
```python
import jax
import jax.numpy as jnp
from jax import lax
from jax.sharding import PartitionSpec as P

HDIM = 64
STEP = 10


NORM_EPS = 1e-05
ROPE_BASE = 10000.0
BLEND = 0.5
BETA_ONE = 0.9
BETA_TWO = 0.999
ADAM_EPS = 1e-06
DECAY = 0.01
MATRIX_RATE = 0.25
GAIN_RATE = 0.7
NEG_LARGE = -1e30


def rope_tables(position_ids, head_dim):
    half_dim = head_dim // 2
    freqs = ROPE_BASE ** (-(jnp.arange(half_dim, dtype=jnp.float32) * 2.0 / head_dim))
    angles = position_ids.astype(jnp.float32)[:, None] * freqs[None, :]
    return (jnp.cos(angles), jnp.sin(angles))


def rotate(vectors, cosine, sine_table, direction_sign):
    half_dim = vectors.shape[-1] // 2
    first_half = vectors[..., :half_dim]
    second_half = vectors[..., half_dim:]
    cos_wide = cosine[:, None, :]
    sin_wide = direction_sign * sine_table[:, None, :]
    return jnp.concatenate(
        [
            first_half * cos_wide - second_half * sin_wide,
            second_half * cos_wide + first_half * sin_wide,
        ],
        axis=-1,
    )


def permitted(segment_ids, is_valid, row_begin, finish):
    query_ids = jnp.arange(row_begin, finish, dtype=jnp.int32)
    key_ids = jnp.arange(finish, dtype=jnp.int32)
    same_doc = segment_ids[row_begin:finish, None] == segment_ids[None, :finish]
    causal = key_ids[None, :] <= query_ids[:, None]
    return same_doc & causal & is_valid[None, :finish] | (key_ids[None, :] == query_ids[:, None])


def attention_forward(queries, keys_rot, values, segment_ids, is_valid):
    length = queries.shape[0]
    block_rows = min(512, length)
    outputs = []
    lse_parts = []
    for block_index in range(length // block_rows):
        row_begin = block_index * block_rows
        finish = row_begin + block_rows
        allowed = permitted(segment_ids, is_valid, row_begin, finish)
        scores = jnp.einsum(
            "qhd,khd->hqk",
            queries[row_begin:finish],
            keys_rot[:finish],
            preferred_element_type=jnp.float32,
        )
        scores = jnp.where(allowed[None], scores, NEG_LARGE)
        row_max = jnp.max(scores, axis=-1, keepdims=True)
        exp_scores = jnp.exp(scores - row_max)
        row_total = jnp.sum(exp_scores, axis=-1, keepdims=True)
        attn_probs = (exp_scores / row_total).astype(jnp.bfloat16)
        mixed = jnp.einsum(
            "hqk,khd->qhd", attn_probs, values[:finish], preferred_element_type=jnp.float32
        )
        outputs.append(mixed.astype(jnp.bfloat16))
        lse_parts.append(row_max + jnp.log(row_total))
    return (jnp.concatenate(outputs, axis=0), lse_parts)


def attention_backward(queries, keys_rot, values, grad_mixed, lse_parts, segment_ids, is_valid):
    length = queries.shape[0]
    block_rows = min(512, length)
    grad_keys = jnp.zeros(keys_rot.shape, jnp.float32)
    grad_values = jnp.zeros(values.shape, jnp.float32)
    grad_query_parts = []
    for block_index in range(length // block_rows):
        row_begin = block_index * block_rows
        finish = row_begin + block_rows
        allowed = permitted(segment_ids, is_valid, row_begin, finish)
        scores = jnp.einsum(
            "qhd,khd->hqk",
            queries[row_begin:finish],
            keys_rot[:finish],
            preferred_element_type=jnp.float32,
        )
        scores = jnp.where(allowed[None], scores, NEG_LARGE)
        attn_probs = jnp.exp(scores - lse_parts[block_index])
        probs_low = attn_probs.astype(jnp.bfloat16)
        grad_block = grad_mixed[row_begin:finish]
        grad_values = grad_values.at[:finish].add(
            jnp.einsum("hqk,qhd->khd", probs_low, grad_block, preferred_element_type=jnp.float32)
        )
        grad_probs = jnp.einsum(
            "qhd,khd->hqk", grad_block, values[:finish], preferred_element_type=jnp.float32
        )
        row_delta = jnp.sum(attn_probs * grad_probs, axis=-1, keepdims=True)
        grad_scores = (attn_probs * (grad_probs - row_delta)).astype(jnp.bfloat16)
        grad_query_parts.append(
            jnp.einsum(
                "hqk,khd->qhd", grad_scores, keys_rot[:finish], preferred_element_type=jnp.float32
            )
        )
        grad_keys = grad_keys.at[:finish].add(
            jnp.einsum(
                "hqk,qhd->khd",
                grad_scores,
                queries[row_begin:finish],
                preferred_element_type=jnp.float32,
            )
        )
    return (jnp.concatenate(grad_query_parts, axis=0), grad_keys, grad_values)


def norm_backward(inputs, inverse, gain, grad_normed):
    scaled = gain * grad_normed
    inner_mean = jnp.mean(scaled * inputs, axis=-1, keepdims=True)
    grad_inputs = inverse * scaled - inputs * inverse**3 * inner_mean
    grad_gain = jnp.sum(grad_normed * inputs * inverse, axis=0)
    return (grad_inputs, grad_gain)


def adam_moments(mean_old, var_old, grad):
    mean_new = BETA_ONE * mean_old + (1.0 - BETA_ONE) * grad
    var_new = BETA_TWO * var_old + (1.0 - BETA_TWO) * grad * grad
    direction = (
        mean_new / (1.0 - BETA_ONE**STEP) / (jnp.sqrt(var_new / (1.0 - BETA_TWO**STEP)) + ADAM_EPS)
    )
    return (mean_new, var_new, direction)


def matrix_step(weight, mean_old, var_old, grad, axes):
    mean_new, var_new, direction = adam_moments(mean_old, var_old, grad)
    update = direction + DECAY * weight
    weight_sq = jnp.sum(weight * weight, axis=axes, keepdims=True)
    update_sq = jnp.sum(update * update, axis=axes, keepdims=True)
    return (mean_new, var_new, update, weight_sq, update_sq)


def per_device(
    tokens_in,
    first_value,
    cotangent,
    counts,
    segments,
    positions,
    norm_gains,
    gain_mean,
    gain_var,
    heads_in,
    heads_in_mean,
    heads_in_var,
    heads_out,
    heads_out_mean,
    heads_out_var,
    gate_up,
    gate_up_mean,
    gate_up_var,
    down_proj,
    down_mean,
    down_var,
):
    in_w, out_w = (
        lax.all_gather(heads_in.astype(jnp.bfloat16), ("seq", "hid"), axis=1, tiled=True),
        lax.all_gather(heads_out.astype(jnp.bfloat16), ("seq", "hid"), axis=1, tiled=True),
    )
    gu_w, down_w = (
        lax.all_gather(gate_up.astype(jnp.bfloat16), ("seq", "heads"), axis=1, tiled=True),
        lax.all_gather(down_proj.astype(jnp.bfloat16), ("seq", "heads"), axis=1, tiled=True),
    )
    own_rows = tokens_in[0].astype(jnp.float32)
    tok_rows, model_width = own_rows.shape
    inv_one = lax.rsqrt(jnp.mean(own_rows * own_rows, axis=-1, keepdims=True) + NORM_EPS)
    normed_one = (own_rows * inv_one * norm_gains[0]).astype(jnp.bfloat16)
    group_rows = lax.all_gather(normed_one, "heads", axis=0, tiled=True)
    length = group_rows.shape[0]
    head_cols = in_w.shape[2]
    heads_here = head_cols // HDIM
    query_scale = HDIM ** (-0.5)
    projected = jnp.einsum("ld,kdc->klc", group_rows, in_w, preferred_element_type=jnp.float32)
    cosine, sine_table = rope_tables(positions[0], HDIM)
    queries = (
        rotate(projected[0].reshape(length, heads_here, HDIM), cosine, sine_table, 1.0)
        * query_scale
    ).astype(jnp.bfloat16)
    keys_rot = rotate(
        projected[1].reshape(length, heads_here, HDIM), cosine, sine_table, 1.0
    ).astype(jnp.bfloat16)
    first_local = first_value[0].astype(jnp.float32)
    blended = (BLEND * projected[2] + (1.0 - BLEND) * first_local).astype(jnp.bfloat16)
    values = blended.reshape(length, heads_here, HDIM)
    segment_ids = segments[0]
    row_ids = jnp.arange(length, dtype=jnp.int32)
    is_valid = row_ids % tok_rows < jnp.repeat(counts[0], tok_rows, total_repeat_length=length)
    attn_mixed, lse_parts = attention_forward(queries, keys_rot, values, segment_ids, is_valid)
    out_flat = attn_mixed.reshape(length, head_cols)
    attn_sum = lax.psum_scatter(
        jnp.dot(out_flat, out_w, preferred_element_type=jnp.float32).astype(jnp.bfloat16),
        "heads",
        scatter_dimension=0,
        tiled=True,
    ).astype(jnp.float32)
    hidden = own_rows + attn_sum
    inv_two = lax.rsqrt(jnp.mean(hidden * hidden, axis=-1, keepdims=True) + NORM_EPS)
    normed_two = (hidden * inv_two * norm_gains[1]).astype(jnp.bfloat16)
    ffn_in, ffn_back = (
        lax.all_gather(normed_two[None], "hid", axis=0, tiled=True),
        lax.all_gather(cotangent, "hid", axis=0, tiled=True),
    )
    ffn_in = ffn_in.reshape(-1, model_width)
    ffn_back = ffn_back.reshape(-1, model_width)
    gate_vals = jnp.einsum("td,kdf->ktf", ffn_in, gu_w, preferred_element_type=jnp.float32)
    gate_sigmoid = jax.nn.sigmoid(gate_vals[0])
    gate_silu = gate_vals[0] * gate_sigmoid
    activation = (gate_silu * gate_vals[1]).astype(jnp.bfloat16)
    ffn_part = jnp.dot(activation, down_w, preferred_element_type=jnp.float32)
    grad_act = jnp.einsum("td,fd->tf", ffn_back, down_w, preferred_element_type=jnp.float32)
    grad_gate = grad_act * gate_vals[1] * gate_sigmoid * (1.0 + gate_vals[0] * (1.0 - gate_sigmoid))
    grad_up = grad_act * gate_silu
    grad_gu_low = jnp.stack([grad_gate, grad_up]).astype(jnp.bfloat16)
    grad_down_w = jnp.einsum("tf,td->fd", activation, ffn_back, preferred_element_type=jnp.float32)
    grad_gu_w = jnp.einsum("td,ktf->kdf", ffn_in, grad_gu_low, preferred_element_type=jnp.float32)
    grad_normed_two = jnp.einsum(
        "ktf,kdf->td", grad_gu_low, gu_w, preferred_element_type=jnp.float32
    )
    ffn_sum, grad_two = (
        lax.psum_scatter(
            ffn_part.astype(jnp.bfloat16), "hid", scatter_dimension=0, tiled=True
        ).astype(jnp.float32),
        lax.psum_scatter(
            grad_normed_two.astype(jnp.bfloat16), "hid", scatter_dimension=0, tiled=True
        ).astype(jnp.float32),
    )
    block_out = (hidden + ffn_sum).astype(jnp.bfloat16)[None]
    grad_norm_two, gain_grad_two = norm_backward(hidden, inv_two, norm_gains[1], grad_two)
    grad_hidden = cotangent[0].astype(jnp.float32) + grad_norm_two
    grad_hidden_low = grad_hidden.astype(jnp.bfloat16)
    gathered_piece = lax.all_gather(grad_hidden_low, "heads", axis=0, tiled=True)
    grad_weight = jnp.einsum(
        "lc,ld->cd", out_flat, gathered_piece, preferred_element_type=jnp.float32
    )
    piece_grad = jnp.einsum("ld,cd->lc", gathered_piece, out_w, preferred_element_type=jnp.float32)
    grad_buffer = piece_grad
    grad_out_w, grad_buffer = (grad_weight, grad_buffer)
    grad_flat = grad_buffer.astype(jnp.bfloat16)
    grad_mixed = grad_flat.reshape(length, heads_here, HDIM)
    grad_queries, grad_keys, grad_values = attention_backward(
        queries, keys_rot, values, grad_mixed, lse_parts, segment_ids, is_valid
    )
    grad_values = grad_values.reshape(length, head_cols)
    first_grad = ((1.0 - BLEND) * grad_values)[None]
    grad_query_raw = rotate(grad_queries * query_scale, cosine, sine_table, -1.0).reshape(
        length, head_cols
    )
    grad_key_raw = rotate(grad_keys, cosine, sine_table, -1.0).reshape(length, head_cols)
    grad_projected = jnp.stack([grad_query_raw, grad_key_raw, BLEND * grad_values]).astype(
        jnp.bfloat16
    )
    grad_in_w = jnp.einsum(
        "ld,klc->kdc", group_rows, grad_projected, preferred_element_type=jnp.float32
    )
    piece_grad = grad_projected
    grad_one = lax.psum_scatter(
        jnp.einsum("klc,kdc->ld", piece_grad, in_w, preferred_element_type=jnp.float32).astype(
            jnp.bfloat16
        ),
        "heads",
        scatter_dimension=0,
        tiled=True,
    ).astype(jnp.float32)
    grad_norm_one, gain_grad_one = norm_backward(own_rows, inv_one, norm_gains[0], grad_one)
    input_grad = (grad_hidden + grad_norm_one)[None]
    in_grad, out_grad = (
        lax.psum_scatter(
            grad_in_w.astype(jnp.bfloat16), ("seq", "hid"), scatter_dimension=1, tiled=True
        ).astype(jnp.float32),
        lax.psum_scatter(
            grad_out_w.astype(jnp.bfloat16), ("seq", "hid"), scatter_dimension=1, tiled=True
        ).astype(jnp.float32),
    )
    gu_grad, down_grad = (
        lax.psum_scatter(grad_gu_w, ("seq", "heads"), scatter_dimension=1, tiled=True),
        lax.psum_scatter(grad_down_w, ("seq", "heads"), scatter_dimension=1, tiled=True),
    )
    in_mean, in_var, in_update, in_wsq, in_usq = matrix_step(
        heads_in, heads_in_mean, heads_in_var, in_grad, (1, 2)
    )
    out_mean, out_var, out_update, out_wsq, out_usq = matrix_step(
        heads_out, heads_out_mean, heads_out_var, out_grad, (0, 1)
    )
    gu_mean, gu_var, gu_update, gu_wsq, gu_usq = matrix_step(
        gate_up, gate_up_mean, gate_up_var, gu_grad, (1, 2)
    )
    dn_mean, dn_var, dn_update, dn_wsq, dn_usq = matrix_step(
        down_proj, down_mean, down_var, down_grad, (0, 1)
    )
    weight_local = jnp.concatenate(
        [in_wsq.reshape(-1), out_wsq.reshape(-1), gu_wsq.reshape(-1), dn_wsq.reshape(-1)]
    )
    update_local = jnp.concatenate(
        [in_usq.reshape(-1), out_usq.reshape(-1), gu_usq.reshape(-1), dn_usq.reshape(-1)]
    )
    blended_wide = blended.astype(jnp.float32)
    value_local = jnp.stack(
        [jnp.sum(first_local * first_local), jnp.sum(blended_wide * blended_wide)]
    )
    gain_local = jnp.stack([gain_grad_one, gain_grad_two])
    gain_grads, weight_tot, update_tot, value_tot = lax.psum(
        (gain_local, weight_local, update_local, value_local), ("seq", "heads", "hid")
    )
    ratios = jnp.sqrt(weight_tot) / jnp.sqrt(update_tot + 1e-12)
    in_new = heads_in - MATRIX_RATE * ratios[0:3].reshape(3, 1, 1) * in_update
    out_new = heads_out - MATRIX_RATE * ratios[3] * out_update
    gu_new = gate_up - MATRIX_RATE * ratios[4:6].reshape(2, 1, 1) * gu_update
    dn_new = down_proj - MATRIX_RATE * ratios[6] * dn_update
    gmean_new, gvar_new, gain_dir = adam_moments(gain_mean, gain_var, gain_grads)
    gains_new = norm_gains - GAIN_RATE * gain_dir
    entries = float(
        length * head_cols * lax.axis_size("seq") * lax.axis_size("heads") * lax.axis_size("hid")
    )
    norms = jnp.concatenate([jnp.sqrt(weight_tot), jnp.sqrt(update_tot)])
    value_norms = jnp.sqrt(value_tot / entries)
    return (
        block_out,
        input_grad,
        first_grad,
        gains_new,
        gmean_new,
        gvar_new,
        in_new,
        in_mean,
        in_var,
        out_new,
        out_mean,
        out_var,
        gu_new,
        gu_mean,
        gu_var,
        dn_new,
        dn_mean,
        dn_var,
        norms,
        value_norms,
    )


def solution(mesh):
    placed = (
        P(("seq", "hid"), "heads", None),
        P(("seq", "hid"), None, "heads"),
        P(("seq", "hid"), "heads", None),
        P(("seq", "hid"), None),
        P(("seq", "hid"), None),
        P(("seq", "hid"), None),
        P(),
        P(),
        P(),
        P(None, ("seq", "hid"), "heads"),
        P(None, ("seq", "hid"), "heads"),
        P(None, ("seq", "hid"), "heads"),
        P("heads", ("seq", "hid")),
        P("heads", ("seq", "hid")),
        P("heads", ("seq", "hid")),
        P(None, ("seq", "heads"), "hid"),
        P(None, ("seq", "heads"), "hid"),
        P(None, ("seq", "heads"), "hid"),
        P("hid", ("seq", "heads")),
        P("hid", ("seq", "heads")),
        P("hid", ("seq", "heads")),
    )
    return jax.shard_map(
        per_device,
        mesh=mesh,
        in_specs=placed,
        out_specs=(
            P(("seq", "hid"), "heads", None),
            P(("seq", "hid"), "heads", None),
            P(("seq", "hid"), None, "heads"),
            P(),
            P(),
            P(),
            P(None, ("seq", "hid"), "heads"),
            P(None, ("seq", "hid"), "heads"),
            P(None, ("seq", "hid"), "heads"),
            P("heads", ("seq", "hid")),
            P("heads", ("seq", "hid")),
            P("heads", ("seq", "hid")),
            P(None, ("seq", "heads"), "hid"),
            P(None, ("seq", "heads"), "hid"),
            P(None, ("seq", "heads"), "hid"),
            P("hid", ("seq", "heads")),
            P("hid", ("seq", "heads")),
            P("hid", ("seq", "heads")),
            P(),
            P(),
        ),
        check_vma=False,
    )
```

profile of v0, /device:TPU:0, one launch (start us, length us, event | category | flops | bytes accessed | tf_op | source)
XLA Modules:
  0.0 946.2 jit_solution(8528399682599636324)
XLA Ops:
  20.5 32.0 %all_gather.26 = bf16[256,1024]{1,0:T(8,128)(2,1)} all-gather(bf16[256,128]{1,0:T(8,128)(2,1)S(1)} %convert_element_type.203), channel_id=1, replica_groups=mesh['seq'=4,'heads'=4,'hid'=2] {'seq','hid'}, dimensions={1}, use_global_device_ids=true | all-gather | bytes 589824 | tf_op jit(solution)/shard_map/all_gather | solution.py:174
  64.3 35.8 %all-gather.9.cloned.1.call-done = bf16[2048,1024]{1,0:T(8,128)(2,1)} async-done(((bf16[512,1024]{1,0:T(8,128)(2,1)}), bf16[2048,1024]{1,0:T(8,128)(2,1)}) %all-gather.9.cloned.1.call-update) | async-done | bytes 4194320 | tf_op jit(solution)/shard_map/all_gather | solution.py:184
  110.2 6.2 select_reduce_fusion.1
  116.4 7.4 select_reduce_fusion
  131.7 7.7 fusion.1
  139.4 6.4 fusion.137
  164.2 42.8 %reduce-scatter.12.cloned.1.call-done = bf16[512,1024]{1,0:T(8,128)(2,1)} async-done(((bf16[2048,1024]{1,0:T(8,128)(2,1)}), bf16[512,1024]{1,0:T(8,128)(2,1)}) %reduce-scatter.12.cloned.1.call-update) | async-done | bytes 1048592 | tf_op jit(solution)/shard_map/reduce_scatter | solution.py:206
  211.9 21.5 %all-gather.13.cloned.1.call-done = bf16[2,1024,1408]{2,1,0:T(8,128)(2,1)} async-done(((bf16[2,64,1408]{2,1,0:T(8,128)(2,1)}), bf16[2,1024,1408]{2,1,0:T(8,128)(2,1)}) %all-gather.13.cloned.1.call-update) | async-done | bytes 5767184 | tf_op jit(solution)/shard_map/all_gather | solution.py:177
  233.4 33.6 %all-gather.21.cloned.1.call-done = bf16[1024,1024]{1,0:T(8,128)(2,1)} async-done(((bf16[512,1024]{1,0:T(8,128)(2,1)}), bf16[1024,1024]{1,0:T(8,128)(2,1)}) %all-gather.21.cloned.1.call-update) | async-done | bytes 2097168 | tf_op jit(solution)/shard_map/all_gather | solution.py:216
  267.0 11.8 %convolution_bitcast_fusion.1 = f32[2,1024,1408]{2,1,0:T(8,128)} fusion(bf16[2,1024,1408]{2,1,0:T(8,128)(2,1)} %all-gather.13.cloned.1.call-done, bf16[1024,1024]{1,0:T(8,128)(2,1)} %all-gather.21.cloned.1.call-done), kind=kOutput, calls=%fused_computation.30 | convolution fusion | flops 5905580032 | bytes 19398656 | tf_op jit(solution)/shard_map/td,kdf->ktf/dot_general | solution.py:221
  278.9 22.6 %all-gather.17.cloned.1.call-done = bf16[2,512,1024]{2,1,0:T(8,128)(2,1)} async-done(((bf16[1,512,1024]{2,1,0:T(8,128)(2,1)}), bf16[2,512,1024]{2,1,0:T(8,128)(2,1)}) %all-gather.17.cloned.1.call-update) | async-done | bytes 2097168 | tf_op jit(solution)/shard_map/all_gather | solution.py:217
  301.5 10.9 %fusion.50 = f32[1408,1024]{0,1:T(8,128)} fusion(bf16[1024,1024]{1,0:T(8,128)(2,1)} %bitcast.302, f32[2,1024,1408]{2,1,0:T(8,128)} %convolution_bitcast_fusion.1), kind=kOutput, calls=%fused_computation.92 | convolution fusion | flops 2961440768 | bytes 19398656 | tf_op jit(solution)/shard_map/tf,td->fd/dot_general | solution.py:230
  312.5 81.5 %reduce-scatter.20.cloned.1.call-done = f32[1408,64]{0,1:T(8,128)} async-done(((f32[1408,1024]{0,1:T(8,128)}), f32[1408,64]{0,1:T(8,128)}) %reduce-scatter.20.cloned.1.call-update) | async-done | bytes 360464 | tf_op jit(solution)/shard_map/reduce_scatter | solution.py:292
  397.2 43.2 %all-gather.15.cloned.1.call-done = bf16[1408,1024]{0,1:T(8,128)(2,1)} async-done(((bf16[1408,64]{0,1:T(8,128)(2,1)}), bf16[1408,1024]{0,1:T(8,128)(2,1)}) %all-gather.15.cloned.1.call-update) | async-done | bytes 2883600 | tf_op jit(solution)/shard_map/all_gather | solution.py:178
  440.4 10.0 %fusion.52 = (bf16[1,1024,1408]{2,1,0:T(8,128)(2,1)S(1)}, bf16[1,1024,1408]{2,1,0:T(8,128)(2,1)S(1)}) fusion(f32[2,1024,1408]{2,1,0:T(8,128)} %convolution_bitcast_fusion.1, bf16[1024,1024]{1,0:T(8,128)(2,1)} %bitcast.303, bf16[1408,1024]{0,1:T(8,128)(2,1)} %all-gather.15.cloned.1.call-done), kind=kOutput, calls=%fused_computation.94 | convolution fusion | flops 2971533312 | bytes 22282240 | tf_op jit(solution)/shard_map/td,fd->tf/dot_general | solution.py:226
  453.0 9.2 bitcast_convert_fusion.1
  462.2 30.5 %reduce-scatter.16.cloned.1.call-done = bf16[512,1024]{1,0:T(8,128)(2,1)} async-done(((bf16[1024,1024]{1,0:T(8,128)(2,1)}), bf16[512,1024]{1,0:T(8,128)(2,1)}) %reduce-scatter.16.cloned.1.call-update) | async-done | bytes 1048592 | tf_op jit(solution)/shard_map/reduce_scatter | solution.py:239
  499.5 12.1 %convolution_bitcast_fusion = f32[2,1024,1408]{1,2,0:T(8,128)} fusion(bf16[1,1024,1408]{2,1,0:T(8,128)(2,1)} %copy-done.74, bf16[1,1024,1408]{2,1,0:T(8,128)(2,1)} %copy-done.73, bf16[1024,1024]{1,0:T(8,128)(2,1)} %all-gather.21.cloned.1.call-done), kind=kOutput, calls=%fused_computation.29 | convolution fusion | flops 5908463616 | bytes 19398656 | tf_op jit(solution)/shard_map/td,ktf->kdf/dot_general | solution.py:231
  511.6 17.8 %copy.111 = f32[2,1024,1408]{2,0,1:T(2,128)} copy(f32[2,1024,1408]{1,2,0:T(8,128)} %convolution_bitcast_fusion) | data formatting | bytes 23068672 | tf_op jit(solution)/shard_map/td,ktf->kdf/transpose | solution.py:231
  555.9 8.0 multiply_reduce_fusion.1
  574.6 6.1 multiply_convert_fusion.2
  580.7 12.9 %multiply_convert_fusion.1 = bf16[4,512,1536]{2,1,0:T(8,128)(2,1)} fusion(f32[4,512,1536]{2,1,0:T(8,128)} %get-tuple-element.291, f32[4,512,1536]{2,1,0:T(8,128)} %get-tuple-element.283, f32[4,512]{1,0:T(4,128)S(1)} %get-tuple-element.290, f32[4,512]{1,0:T(4,128)S(1)} %log_add_fusion.1, pred[512,1536]{1,0:T(8,128)(4,1)S(1)} %fusion.46), kind=kLoop, calls=%fused_computation.7 | loop fusion | flops 15728640 | bytes 32260096 | tf_op jit(solution)/shard_map/convert_element_type | solution.py:107
  594.6 7.5 fusion.72
  631.5 11.1 %multiply_reduce_fusion = (f32[4,512]{1,0:T(4,128)}, f32[4,512,2048]{2,1,0:T(8,128)}) fusion(f32[4,512,2048]{2,1,0:T(8,128)S(1)} %bitcast.250, f32[4,512]{1,0:T(4,128)S(1)} %log_add_fusion, pred[512,2048]{1,0:T(8,128)(4,1)S(1)} %fusion.36, bf16[512,4,64]{0,2,1:T(8,128)(2,1)} %bitcast.270, bf16[2048,4,64]{0,2,1:T(8,128)(2,1)} %bitcast.258), kind=kOutput, calls=%fused_computation.1 | convolution fusion | flops 553646080 | bytes 35930112 | tf_op jit(solution)/shard_map/qhd,khd->hqk/dot_general | solution.py:103
  642.6 9.2 multiply_convert_fusion
  663.1 7.2 fusion.114
  675.1 7.5 bitcast_convert_fusion
  687.9 10.2 %fusion.108 = bf16[1024,1024]{1,0:T(8,128)(2,1)} fusion(bf16[1408,1024]{0,1:T(8,128)(2,1)} %all-gather.15.cloned.1.call-done, f32[2,1024,1408]{2,1,0:T(8,128)} %convolution_bitcast_fusion.1), kind=kOutput, calls=%fused_computation.153 | convolution fusion | flops 2962489344 | bytes 16515072 | tf_op jit(solution)/shard_map/dot_general | solution.py:225
  698.1 51.8 %all-reduce.6.cloned.1.call-done = f32[2,1024,1408]{2,0,1:T(2,128)} async-done(((f32[2,1024,1408]{2,0,1:T(2,128)}), f32[2,1024,1408]{2,0,1:T(2,128)}) %all-reduce.6.cloned.1.call-update) | async-done | bytes 11534352
  760.9 63.1 %reduce-scatter.22.cloned.1.call-done = bf16[128,768]{1,0:T(8,128)(2,1)} async-done(((bf16[1024,768]{1,0:T(8,128)(2,1)}), bf16[128,768]{1,0:T(8,128)(2,1)}) %reduce-scatter.22.cloned.1.call-update) | async-done | bytes 196624
  830.4 39.6 %reduce-scatter.18.cloned.1.call-done = bf16[512,1024]{1,0:T(8,128)(2,1)} async-done(((bf16[2048,1024]{1,0:T(8,128)(2,1)}), bf16[512,1024]{1,0:T(8,128)(2,1)}) %reduce-scatter.18.cloned.1.call-update) | async-done | bytes 1048592 | tf_op jit(solution)/shard_map/reduce_scatter | solution.py:272
  874.2 39.9 %all-reduce.3 = (f32[2,1024]{1,0:T(2,128)}, f32[7]{0:T(128)}, f32[7]{0:T(128)}, f32[2]{0:T(128)}) all-reduce(f32[2,1024]{1,0:T(2,128)} %pad_maximum_fusion.15, f32[7]{0:T(128)} %pad_maximum_fusion.17, f32[7]{0:T(128)} %pad_maximum_fusion.16, f32[2]{0:T(128)} %pad_maximum_fusion.19), channel_id=1, replica_groups=mesh['seq'=4,'heads'=4,'hid'=2] {'seq','heads','hid'}, use_global_device_ids=true, to_apply=%region_22.23 | all-reduce | flops 2064 | bytes 16512 | tf_op jit(solution)/shard_map/psum | solution.py:317
  (345 shorter events, 210.2 us)
Async XLA Ops:
  8.1 56.2 %all-gather.11.cloned.1.call-start = ((), (), s32[]{:S(2)}) async-start(), calls=%async_computation.8 | async-start | bytes 1769472 | tf_op jit(solution)/shard_map/all_gather | solution.py:173
  10.2 89.9 %all-gather.9.cloned.1.call-start = ((), (), s32[]{:S(2)}) async-start(), calls=%async_computation.7 | async-start | bytes 5242880 | tf_op jit(solution)/shard_map/all_gather | solution.py:184
  13.1 482.6 %copy-start.55 = (f32[1,1024]{1,0:T(1,128)}, f32[1,1024]{1,0:T(1,128)S(1)}, u32[]{:S(2)}) copy-start(f32[1,1024]{1,0:T(1,128)S(1)} %get-tuple-element.261) | copy-start | bytes 12292
  15.6 191.4 %reduce-scatter.12.cloned.1.call-start = ((), (), s32[]{:S(2)}) async-start(), calls=%async_computation.9 | async-start | bytes 5242880 | tf_op jit(solution)/shard_map/reduce_scatter | solution.py:206
  52.8 72.7 %copy-start.22 = (pred[512,512]{0,1:T(8,128)(4,1)}, pred[512,512]{0,1:T(8,128)(4,1)S(1)}, u32[]{:S(2)}) copy-start(pred[512,512]{0,1:T(8,128)(4,1)S(1)} %fusion.142) | copy-start | bytes 786436
  53.7 75.3 %copy-start.13 = (pred[512,1024]{1,0:T(8,128)(4,1)}, pred[512,1024]{1,0:T(8,128)(4,1)S(1)}, u32[]{:S(2)}) copy-start(pred[512,1024]{1,0:T(8,128)(4,1)S(1)} %fusion.105) | copy-start | bytes 1572868
  107.7 45.1 %copy-start.18 = (bf16[1,2048,256]{1,2,0:T(8,128)(2,1)}, bf16[1,2048,256]{1,2,0:T(8,128)(2,1)S(1)}, u32[]{:S(2)}) copy-start(bf16[1,2048,256]{1,2,0:T(8,128)(2,1)S(1)} %get-tuple-element.237) | copy-start | bytes 3145732
  162.1 44.9 %copy-start.3 = (bf16[1,512,1024]{2,1,0:T(8,128)(2,1)S(1)}, bf16[1,512,1024]{2,1,0:T(8,128)(2,1)}, u32[]{:S(2)}) copy-start(bf16[1,512,1024]{2,1,0:T(8,128)(2,1)} %param.43) | copy-start | bytes 3145732
  162.1 71.3 %all-gather.13.cloned.1.call-start = ((), (), s32[]{:S(2)}) async-start(), calls=%async_computation.10 | async-start | bytes 6127616 | tf_op jit(solution)/shard_map/all_gather | solution.py:177
  164.1 102.9 %all-gather.21.cloned.1.call-start = ((), (), s32[]{:S(2)}) async-start(), calls=%async_computation.18 | async-start | bytes 3145728 | tf_op jit(solution)/shard_map/all_gather | solution.py:216
  208.7 287.0 %copy-start.60 = (f32[512]{0:T(512)}, f32[512]{0:T(512)S(1)}, u32[]{:S(2)}) copy-start(f32[512]{0:T(512)S(1)} %get-tuple-element.270) | copy-start | bytes 6148
  208.7 287.0 %copy-start.64 = (f32[512]{0:T(512)}, f32[512]{0:T(512)S(1)}, u32[]{:S(2)}) copy-start(f32[512]{0:T(512)S(1)} %get-tuple-element.269) | copy-start | bytes 6148
  211.3 90.2 %all-gather.17.cloned.1.call-start = ((), (), s32[]{:S(2)}) async-start(), calls=%async_computation.13 | async-start | bytes 3145728 | tf_op jit(solution)/shard_map/all_gather | solution.py:217
  211.9 182.1 %reduce-scatter.20.cloned.1.call-start = ((), (), s32[]{:S(2)}) async-start(), calls=%async_computation.17 | async-start | bytes 6127616 | tf_op jit(solution)/shard_map/reduce_scatter | solution.py:292
  312.4 128.0 %all-gather.15.cloned.1.call-start = ((), (), s32[]{:S(2)}) async-start(), calls=%async_computation.11 | async-start | bytes 3063808 | tf_op jit(solution)/shard_map/all_gather | solution.py:178
  397.2 95.5 %reduce-scatter.16.cloned.1.call-start = ((), (), s32[]{:S(2)}) async-start(), calls=%async_computation.14 | async-start | bytes 3145728 | tf_op jit(solution)/shard_map/reduce_scatter | solution.py:239
  462.2 71.8 %all-gather.19.cloned.1.call-start = ((), (), s32[]{:S(2)}) async-start(), calls=%async_computation.15 | async-start | bytes 5242880 | tf_op jit(solution)/shard_map/all_gather | solution.py:247
  499.4 250.6 %all-reduce.6.cloned.1.call-start = ((), (), s32[]{:S(2)}) async-start(), calls=%async_computation.21 | async-start | bytes 23068672
  529.4 226.3 %reduce-scatter.24.cloned.1.call-start = ((), (), s32[]{:S(2)}) async-start(), calls=%async_computation.20 | async-start | bytes 589824
  657.9 166.2 %reduce-scatter.22.cloned.1.call-start = ((), (), s32[]{:S(2)}) async-start(), calls=%async_computation.19 | async-start | bytes 1769472
  675.0 195.0 %reduce-scatter.18.cloned.1.call-start = ((), (), s32[]{:S(2)}) async-start(), calls=%async_computation.16 | async-start | bytes 5242880 | tf_op jit(solution)/shard_map/reduce_scatter | solution.py:272
  682.6 251.7 %reduce-scatter.14.cloned.1.call-start = ((), (), s32[]{:S(2)}) async-start(), calls=%async_computation.12 | async-start | bytes 3145728 | tf_op jit(solution)/shard_map/reduce_scatter | solution.py:236
  687.9 63.2 %copy-start.26 = (f32[2,64,1408]{2,1,0:T(8,128)S(1)}, f32[2,64,1408]{2,1,0:T(8,128)}, u32[]{:S(2)}) copy-start(f32[2,64,1408]{2,1,0:T(8,128)} %param.58) | copy-start | bytes 2162692
  698.1 58.6 %copy-start.45 = (f32[256,128]{1,0:T(8,128)S(1)}, f32[256,128]{1,0:T(8,128)}, u32[]{:S(2)}) copy-start(f32[256,128]{1,0:T(8,128)} %param.55) | copy-start | bytes 393220
  698.1 127.1 %copy-start.28 = (f32[3,128,256]{1,2,0:T(8,128)S(1)}, f32[3,128,256]{1,2,0:T(8,128)}, u32[]{:S(2)}) copy-start(f32[3,128,256]{1,2,0:T(8,128)} %copy-done.27) | copy-start | bytes 1179652
  751.1 118.9 %copy-start.4 = (bf16[1,512,1024]{2,1,0:T(8,128)(2,1)S(1)}, bf16[1,512,1024]{2,1,0:T(8,128)(2,1)}, u32[]{:S(2)}) copy-start(bf16[1,512,1024]{2,1,0:T(8,128)(2,1)} %param.43) | copy-start | bytes 3145732
  751.2 118.9 %copy-start.59 = (f32[1,1024]{1,0:T(1,128)S(1)}, f32[1,1024]{1,0:T(1,128)}, u32[]{:S(2)}) copy-start(f32[1,1024]{1,0:T(1,128)} %copy-done.58) | copy-start | bytes 12292
  751.2 118.9 %copy-start.63 = (f32[512]{0:T(512)S(1)}, f32[512]{0:T(512)}, u32[]{:S(2)}) copy-start(f32[512]{0:T(512)} %copy-done.62) | copy-start | bytes 6148
  872.7 61.6 %copy-start.12 = (bf16[512,1024]{1,0:T(8,128)(2,1)S(1)}, bf16[512,1024]{1,0:T(8,128)(2,1)}, u32[]{:S(2)}) copy-start(bf16[512,1024]{1,0:T(8,128)(2,1)} %reduce-scatter.12.cloned.1.call-done) | copy-start | bytes 3145732
  872.7 61.6 %copy-start.21 = (bf16[1,512,1024]{2,1,0:T(8,128)(2,1)S(1)}, bf16[1,512,1024]{2,1,0:T(8,128)(2,1)}, u32[]{:S(2)}) copy-start(bf16[1,512,1024]{2,1,0:T(8,128)(2,1)} %param.45) | copy-start | bytes 3145732
  872.7 61.6 %copy-start.56 = (f32[1,1024]{1,0:T(1,128)S(1)}, f32[1,1024]{1,0:T(1,128)}, u32[]{:S(2)}) copy-start(f32[1,1024]{1,0:T(1,128)} %copy-done.55) | copy-start | bytes 12292
  872.7 61.6 %copy-start.61 = (f32[512]{0:T(512)S(1)}, f32[512]{0:T(512)}, u32[]{:S(2)}) copy-start(f32[512]{0:T(512)} %copy-done.60) | copy-start | bytes 6148
  (78 other events, 752.7 us)
Sparse Core Ops, SparseCore 0:
  11.6 52.6 all-gather.10
  66.4 33.5 all-gather.8
  162.2 44.7 reduce-scatter.11
  499.5 34.4 all-gather.18
  658.0 97.6 reduce-scatter.23
  759.3 64.6 reduce-scatter.21
  826.5 43.4 reduce-scatter.17
  872.9 32.4 reduce-scatter.13
Sparse Core Ops, SparseCore 1:
  165.7 67.6 all-gather.12
  235.5 31.5 all-gather.20
  268.5 32.9 all-gather.16
  312.5 81.4 reduce-scatter.19
  397.2 43.1 all-gather.14
  462.2 30.4 reduce-scatter.15
  529.5 220.4 all-reduce.5
where the time goes:
time: 951 us; the launch traced here: 946 us
  waiting for transfers between devices  476 us (50%)
  matrix products  198 us (21%)
  other arithmetic  122 us (13%)
  blocking collectives  71.9 us (8%)
  local copies, waits for them, and re-layouts  58 us (6%)
  between operations  19.1 us (2%)
    unnamed x18, waiting for transfers between devices  117 us
    reduce_scatter x1, waiting for transfers between devices, per_device(): lax.psum_scatter(grad_down_w, ('seq', 'heads'), scatter_dimension=1, tile...  81.5 us
    all_gather x1, waiting for transfers between devices, per_device(): lax.all_gather(down_proj.astype(jnp.bfloat16), ('seq', 'heads'), axis=1,...  43.2 us
    reduce_scatter x1, waiting for transfers between devices, per_device(): lax.psum_scatter(jnp.dot(out_flat, out_w, preferred_element_type=jnp.floa...  42.8 us
    psum x1, blocking collectives, per_device(): lax.psum((gain_local, weight_local, update_local, value_local), ('seq', '...  39.9 us
    reduce_scatter x1, waiting for transfers between devices, per_device(): lax.psum_scatter(jnp.einsum('klc,kdc->ld', piece_grad, in_w, preferred_el...  39.6 us
    all_gather x1, waiting for transfers between devices, per_device(): group_rows = lax.all_gather(normed_one, 'heads', axis=0, tiled=True)  35.8 us
    all_gather x1, waiting for transfers between devices, per_device(): lax.all_gather(normed_two[None], 'hid', axis=0, tiled=True)  33.6 us
  transfers between devices with their start and end apart: 15, of which 14 were waited for; matrix products, arithmetic and copies ran while one was open for 28% of the time, Pallas kernels for 0%

commit v1 on v0

v1 whole, which is shorter than its diff:
```python
import functools

import jax
import jax.numpy as jnp
from jax import lax
from jax.experimental import pallas as pl
from jax.experimental.pallas import tpu as pltpu
from jax.sharding import PartitionSpec as P

HDIM = 64
STEP = 10


NORM_EPS = 1e-05
ROPE_BASE = 10000.0
BLEND = 0.5
BETA_ONE = 0.9
BETA_TWO = 0.999
ADAM_EPS = 1e-06
DECAY = 0.01
MATRIX_RATE = 0.25
GAIN_RATE = 0.7
NEG_LARGE = -1e30

BLOCK = 512
EXTRA = 16
SEGMENTS = 3
NN = ((1,), (0,))
NT = ((1,), (1,))
TN = ((0,), (0,))
F32 = jnp.float32
LOW = jnp.bfloat16


def dot(left, right, dims):
    return lax.dot_general(left, right, (dims, ((), ())), preferred_element_type=F32)


def tile_plan(length, block):
    tiles = []
    half = block // 2
    for begin in range(0, length, block):
        tiles.append((begin, half, begin, half, True))
        tiles.append((begin + half, half, begin, block, True))
        for key_begin in range(0, begin, block):
            tiles.append((begin, block, key_begin, block, False))
    return tiles


def diagonal_mask(scores, query_segs, key_segs, query_begin, key_begin):
    rows = lax.broadcasted_iota(jnp.int32, scores.shape, 0) + key_begin
    cols = lax.broadcasted_iota(jnp.int32, scores.shape, 1) + query_begin
    allowed = ((key_segs == query_segs) & (rows <= cols)) | (rows == cols)
    return jnp.where(allowed, scores, NEG_LARGE)


def segment_rows(query_segs, key_segs):
    shape = (EXTRA, query_segs.shape[1])
    row_ids = lax.broadcasted_iota(jnp.int32, shape, 0)
    query_rows = jnp.where(row_ids == query_segs, 1.0, 0.0)
    key_rows = jnp.where((row_ids < SEGMENTS) & (row_ids != key_segs), NEG_LARGE, 0.0)
    return (row_ids, query_rows, key_rows)


def attend_kernel(
    block, q_ref, k_ref, v_ref, qseg_ref, kseg_ref, ksegrow_ref, out_ref, lse_ref, q_ext, k_ext, v_ext
):
    length = q_ref.shape[1]
    row_ids, query_rows, key_rows = segment_rows(qseg_ref[...], ksegrow_ref[...])
    q_ext[0:HDIM, :] = q_ref[...]
    k_ext[0:HDIM, :] = k_ref[...]
    v_ext[0:HDIM, :] = v_ref[...]
    q_ext[HDIM:, :] = query_rows.astype(LOW)
    k_ext[HDIM:, :] = key_rows.astype(LOW)
    v_ext[HDIM:, :] = jnp.where(row_ids == 0, 1.0, 0.0).astype(LOW)
    tiles = tile_plan(length, block)

    def score(tile):
        q0, qn, k0, kn, diagonal = tile
        if diagonal:
            return dot(k_ref[:, k0 : k0 + kn], q_ref[:, q0 : q0 + qn], TN)
        return dot(k_ext[:, k0 : k0 + kn], q_ext[:, q0 : q0 + qn], TN)

    ahead = score(tiles[0])
    halves = []
    state = None
    for index, (q0, qn, k0, kn, diagonal) in enumerate(tiles):
        scores = ahead
        if index + 1 < len(tiles):
            ahead = score(tiles[index + 1])
        if diagonal:
            scores = diagonal_mask(
                scores, qseg_ref[:, q0 : q0 + qn], kseg_ref[k0 : k0 + kn, :], q0, k0
            )
        new_max = jnp.max(scores, axis=0, keepdims=True)
        if not diagonal:
            new_max = jnp.maximum(state[0], new_max)
        probs = jnp.exp(scores - new_max).astype(LOW)
        mixed = dot(v_ext[:, k0 : k0 + kn], probs, NN)
        if diagonal:
            halves.append((new_max, mixed))
            if len(halves) == 2:
                state = tuple(jnp.concatenate(pair, axis=1) for pair in zip(*halves))
                halves = []
        else:
            state = (new_max, state[1] * jnp.exp(state[0] - new_max) + mixed)
        if index + 1 == len(tiles) or (tiles[index + 1][4] and not halves):
            total = state[1][HDIM : HDIM + 1, :]
            begin = (q0 // block) * block
            out_ref[:, begin : begin + block] = (state[1][0:HDIM, :] / total).astype(LOW)
            lse_ref[0, :, begin : begin + block] = state[0] + jnp.log(total)


def head_specs(length):
    return (
        pl.BlockSpec((HDIM, length), lambda head: (head, 0)),
        pl.BlockSpec((1, length), lambda head: (0, 0)),
        pl.BlockSpec((length, 1), lambda head: (0, 0)),
        pl.BlockSpec((1, 1, length), lambda head: (head, 0, 0)),
    )


def attention_forward(queries, keys_rot, values, query_segs, key_segs):
    cols, length = queries.shape
    heads = cols // HDIM
    wide, row, column, per_head = head_specs(length)
    return pl.pallas_call(
        functools.partial(attend_kernel, min(BLOCK, length)),
        grid=(heads,),
        in_specs=[wide, wide, wide, row, column, row],
        out_specs=[wide, per_head],
        out_shape=[
            jax.ShapeDtypeStruct((cols, length), LOW),
            jax.ShapeDtypeStruct((heads, 1, length), F32),
        ],
        scratch_shapes=[pltpu.VMEM((HDIM + EXTRA, length), LOW)] * 3,
        compiler_params=pltpu.CompilerParams(vmem_limit_bytes=40 << 20),
        cost_estimate=pl.CostEstimate(
            flops=8 * cols * length * length,
            bytes_accessed=8 * cols * length,
            transcendentals=heads * length * length,
        ),
    )(queries, keys_rot, values, query_segs, key_segs.reshape(length, 1), key_segs)


def three_terms(value):
    high = value.astype(LOW).astype(F32)
    middle = (value - high).astype(LOW).astype(F32)
    return (high, middle, value - high - middle)


def attend_back_kernel(
    block,
    q_ref,
    k_ref,
    v_ref,
    grad_ref,
    out_ref,
    lse_ref,
    qseg_ref,
    kseg_ref,
    ksegrow_ref,
    dq_ref,
    dk_ref,
    dv_ref,
    q_ext,
    k_ext,
    v_ext,
    g_ext,
):
    length = q_ref.shape[1]
    half = block // 2
    row_ids, query_rows, key_rows = segment_rows(qseg_ref[...], ksegrow_ref[...])
    delta = jnp.sum(grad_ref[...].astype(F32) * out_ref[...].astype(F32), axis=0, keepdims=True)
    for row, term in enumerate(three_terms(-lse_ref[0])):
        query_rows = jnp.where(row_ids == SEGMENTS + row, term, query_rows)
    key_rows = jnp.where((row_ids >= SEGMENTS) & (row_ids < SEGMENTS + 3), 1.0, key_rows)
    grad_rows = jnp.zeros_like(query_rows)
    for row, term in enumerate(three_terms(-delta)):
        grad_rows = jnp.where(row_ids == row, term, grad_rows)
    q_ext[0:HDIM, :] = q_ref[...]
    k_ext[0:HDIM, :] = k_ref[...]
    v_ext[0:HDIM, :] = v_ref[...]
    g_ext[0:HDIM, :] = grad_ref[...]
    q_ext[HDIM:, :] = query_rows.astype(LOW)
    k_ext[HDIM:, :] = key_rows.astype(LOW)
    v_ext[HDIM:, :] = jnp.where(row_ids < 3, 1.0, 0.0).astype(LOW)
    g_ext[HDIM:, :] = grad_rows.astype(LOW)
    tiles = tile_plan(length, block)

    def score(tile):
        q0, qn, k0, kn, diagonal = tile
        rows, cols = slice(k0, k0 + kn), slice(q0, q0 + qn)
        if diagonal:
            scores = dot(k_ref[:, rows], q_ref[:, cols], TN)
        else:
            scores = dot(k_ext[:, rows], q_ext[:, cols], TN)
        return (scores, dot(v_ext[:, rows], g_ext[:, cols], TN))

    ahead = score(tiles[0])
    for index, (q0, qn, k0, kn, diagonal) in enumerate(tiles):
        scores, grad_probs = ahead
        if index + 1 < len(tiles):
            ahead = score(tiles[index + 1])
        rows, cols = slice(k0, k0 + kn), slice(q0, q0 + qn)
        if diagonal:
            scores = diagonal_mask(scores, qseg_ref[:, cols], kseg_ref[rows, :], q0, k0)
            scores = scores - lse_ref[0, :, cols]
        probs = jnp.exp(scores)
        grad_scores = (probs * grad_probs).astype(LOW)
        dv = dot(grad_ref[:, cols], probs.astype(LOW), NT)
        dk = dot(q_ref[:, cols], grad_scores, NT)
        dq = dot(k_ref[:, rows], grad_scores, NN)
        if not diagonal:
            dq_ref[:, cols] += dq
            dk_ref[:, rows] += dk
            dv_ref[:, rows] += dv
            continue
        dq_ref[:, cols] = dq
        if kn == half:
            dk_ref[:, rows] = dk
            dv_ref[:, rows] = dv
        else:
            low_rows, high_rows = slice(k0, k0 + half), slice(k0 + half, k0 + block)
            dk_ref[:, low_rows] += dk[:, :half]
            dv_ref[:, low_rows] += dv[:, :half]
            dk_ref[:, high_rows] = dk[:, half:]
            dv_ref[:, high_rows] = dv[:, half:]


def attention_backward(queries, keys_rot, values, grad_mixed, mixed, lse, query_segs, key_segs):
    cols, length = queries.shape
    heads = cols // HDIM
    wide, row, column, per_head = head_specs(length)
    return pl.pallas_call(
        functools.partial(attend_back_kernel, min(BLOCK, length)),
        grid=(heads,),
        in_specs=[wide] * 5 + [per_head, row, column, row],
        out_specs=[wide] * 3,
        out_shape=[jax.ShapeDtypeStruct((cols, length), F32)] * 3,
        scratch_shapes=[pltpu.VMEM((HDIM + EXTRA, length), LOW)] * 4,
        compiler_params=pltpu.CompilerParams(vmem_limit_bytes=40 << 20),
        cost_estimate=pl.CostEstimate(
            flops=20 * cols * length * length,
            bytes_accessed=22 * cols * length,
            transcendentals=heads * length * length,
        ),
    )(
        queries,
        keys_rot,
        values,
        grad_mixed,
        mixed,
        lse,
        query_segs,
        key_segs.reshape(length, 1),
        key_segs,
    )


def swap(value, axis, mask):
    return lax.ppermute(value, axis, [(i, i ^ mask) for i in range(lax.axis_size(axis))])


def ring(value, axis):
    size = lax.axis_size(axis)
    return lax.ppermute(value, axis, [(i, (i + 1) % size) for i in range(size)])


def masks_from_high(size):
    bit = size // 2
    while bit:
        yield bit
        bit //= 2


def gather_masks(value, axis, bits):
    held = {0: value}
    for bit in bits:
        held.update({mask ^ bit: swap(block, axis, bit) for mask, block in list(held.items())})
    return held


def total(value, axis):
    size = lax.axis_size(axis)
    bit = 1
    while bit < size:
        if bit * 4 <= size:
            one, two, three = (swap(value, axis, mask * bit) for mask in (1, 2, 3))
            value = (value + one) + (two + three)
            bit *= 4
        else:
            value = value + swap(value, axis, bit)
            bit *= 2
    return value


def after(value, other):
    return lax.optimization_barrier((value, other))[0]


def take(value, index, size, axis):
    return lax.dynamic_slice_in_dim(value, index * size, size, axis)


def put(buffer, value, index, axis):
    return lax.dynamic_update_slice_in_dim(buffer, value, index * value.shape[axis], axis)


def ring_scatter(block_of, axis):
    size = lax.axis_size(axis)
    me = lax.axis_index(axis)
    value = block_of(lax.rem(me + size - 1, size))
    for step in range(1, size):
        moved = ring(value.astype(LOW), axis)
        value = moved.astype(F32) + block_of(lax.rem(me + 2 * size - 1 - step, size))
    return value


def norm_backward(inputs, inverse, gain, grad_normed):
    scaled = gain * grad_normed
    inner_mean = jnp.mean(scaled * inputs, axis=-1, keepdims=True)
    grad_inputs = inverse * scaled - inputs * inverse**3 * inner_mean
    grad_gain = jnp.sum(grad_normed * inputs * inverse, axis=0)
    return (grad_inputs, grad_gain)


def adam_moments(mean_old, var_old, grad):
    mean_new = BETA_ONE * mean_old + (1.0 - BETA_ONE) * grad
    var_new = BETA_TWO * var_old + (1.0 - BETA_TWO) * grad * grad
    direction = (
        mean_new / (1.0 - BETA_ONE**STEP) / (jnp.sqrt(var_new / (1.0 - BETA_TWO**STEP)) + ADAM_EPS)
    )
    return (mean_new, var_new, direction)


def matrix_step(weight, mean_old, var_old, grad, axes):
    mean_new, var_new, direction = adam_moments(mean_old, var_old, grad)
    update = direction + DECAY * weight
    weight_sq = jnp.sum(weight * weight, axis=axes, keepdims=True)
    update_sq = jnp.sum(update * update, axis=axes, keepdims=True)
    return (mean_new, var_new, update, weight_sq, update_sq)


def rope_tables(position_ids):
    half_dim = HDIM // 2
    freqs = ROPE_BASE ** (-(jnp.arange(half_dim, dtype=jnp.float32) * 2.0 / HDIM))
    angles = freqs[:, None] * position_ids.astype(jnp.float32)[None, :]
    return (jnp.cos(angles), jnp.sin(angles))


def rotate(vectors, cosine, sine_table, direction_sign):
    cols, length = vectors.shape
    halves = vectors.reshape(cols // HDIM, 2, HDIM // 2, length)
    first_half, second_half = halves[:, 0], halves[:, 1]
    sine = direction_sign * sine_table
    return jnp.stack(
        [
            first_half * cosine - second_half * sine,
            second_half * cosine + first_half * sine,
        ],
        axis=1,
    ).reshape(cols, length)


def per_device(
    tokens_in,
    first_value,
    cotangent,
    counts,
    segments,
    positions,
    norm_gains,
    gain_mean,
    gain_var,
    heads_in,
    heads_in_mean,
    heads_in_var,
    heads_out,
    heads_out_mean,
    heads_out_var,
    gate_up,
    gate_up_mean,
    gate_up_var,
    down_proj,
    down_mean,
    down_var,
):
    n_seq, n_heads, n_hid = (lax.axis_size(name) for name in ("seq", "heads", "hid"))
    at_seq, at_heads, at_hid = (lax.axis_index(name) for name in ("seq", "heads", "hid"))
    own_rows = tokens_in[0].astype(F32)
    tok_rows, model_width = own_rows.shape
    length = tok_rows * n_heads
    head_cols = heads_in.shape[2]
    hidden_cols = gate_up.shape[2]
    query_scale = HDIM ** (-0.5)
    far_bits = [bit for bit in masks_from_high(n_heads) if bit > 1]
    near = 1

    inv_one = lax.rsqrt(jnp.mean(own_rows * own_rows, axis=-1, keepdims=True) + NORM_EPS)
    normed_one = (own_rows * inv_one * norm_gains[0]).astype(LOW)
    row_blocks = gather_masks(normed_one, "heads", far_bits)
    far_rows = row_blocks[n_heads // 2]
    row_blocks.update(
        {mask ^ near: swap(block, "heads", near) for mask, block in list(row_blocks.items())}
    )
    group_rows = jnp.zeros((length, model_width), LOW)
    for mask, block in row_blocks.items():
        group_rows = put(group_rows, block, at_heads ^ mask, 0)

    in_low = jnp.swapaxes(heads_in, 1, 2).astype(LOW)
    out_low = heads_out.astype(LOW)
    out_parts = gather_masks(out_low, "heads", far_bits)
    out_masks = list(out_parts)
    piece = jnp.concatenate([in_low] + [out_parts[mask][None] for mask in out_masks], axis=0)
    head_weights = jnp.zeros((piece.shape[0], head_cols, model_width), LOW)
    for step in range(n_seq):
        if step:
            piece = ring(piece, "seq")
        from_seq = lax.rem(at_seq + n_seq - step, n_seq)
        for mask, block in gather_masks(piece, "hid", masks_from_high(n_hid)).items():
            head_weights = put(head_weights, block, from_seq * n_hid + (at_hid ^ mask), 2)
    last_piece = piece
    in_w = head_weights[:3].reshape(3 * head_cols, model_width)
    out_here = head_weights[3:]
    out_near = swap(out_here, "heads", near)
    out_w = jnp.zeros((n_heads * head_cols, model_width), LOW)
    for slot, mask in enumerate(out_masks):
        out_w = put(out_w, out_here[slot], at_heads ^ mask, 0)
        out_w = put(out_w, out_near[slot], at_heads ^ mask ^ near, 0)

    ffn_piece = jnp.concatenate(
        [gate_up.astype(LOW), jnp.swapaxes(down_proj, 0, 1).astype(LOW)[None]], axis=0
    )
    ffn_piece = after(ffn_piece, last_piece)
    ffn_w = jnp.zeros((3, model_width, hidden_cols), LOW)
    for step in range(n_seq):
        if step:
            ffn_piece = ring(ffn_piece, "seq")
        from_seq = lax.rem(at_seq + n_seq - step, n_seq)
        blocks = gather_masks(after(ffn_piece, far_rows), "heads", masks_from_high(n_heads))
        for mask, block in blocks.items():
            ffn_w = put(ffn_w, block, from_seq * n_heads + (at_heads ^ mask), 1)

    projected = dot(in_w, group_rows, NT).reshape(3, head_cols, length)
    cosine, sine_table = rope_tables(positions[0])
    queries = (rotate(projected[0], cosine, sine_table, 1.0) * query_scale).astype(LOW)
    keys_rot = rotate(projected[1], cosine, sine_table, 1.0).astype(LOW)
    first_local = first_value[0].T.astype(F32)
    values = (BLEND * projected[2] + (1.0 - BLEND) * first_local).astype(LOW)
    row_ids = jnp.arange(length, dtype=jnp.int32)
    is_valid = row_ids % tok_rows < jnp.repeat(counts[0], tok_rows, total_repeat_length=length)
    query_segs = segments
    key_segs = jnp.where(is_valid[None], segments, -1)
    mixed, lse = attention_forward(queries, keys_rot, values, query_segs, key_segs)

    mixed_own = jnp.zeros((n_heads * head_cols, tok_rows), LOW)
    mixed_own = put(mixed_own, take(mixed, at_heads, tok_rows, 1), at_heads, 0)
    for mask in range(n_heads - 1, 0, -1):
        block = swap(take(mixed, at_heads ^ mask, tok_rows, 1), "heads", mask)
        mixed_own = put(mixed_own, block, at_heads ^ mask, 0)
    hidden = own_rows + dot(mixed_own, out_w, TN)
    inv_two = lax.rsqrt(jnp.mean(hidden * hidden, axis=-1, keepdims=True) + NORM_EPS)
    normed_two = (hidden * inv_two * norm_gains[1]).astype(LOW)

    back_other = swap(after(cotangent[0], last_piece), "hid", 1)
    ffn_in = jnp.concatenate([normed_two, swap(normed_two, "hid", 1)], axis=0)
    ffn_back = jnp.concatenate([cotangent[0], back_other], axis=0)
    gate_vals = dot(ffn_in, ffn_w[0], NN)
    up_vals = dot(ffn_in, ffn_w[1], NN)
    grad_act = dot(ffn_back, ffn_w[2], NN)
    gate_sigmoid = jax.nn.sigmoid(gate_vals)
    gate_silu = gate_vals * gate_sigmoid
    activation = (gate_silu * up_vals).astype(LOW)
    grad_gate = (
        grad_act * up_vals * gate_sigmoid * (1.0 + gate_vals * (1.0 - gate_sigmoid))
    ).astype(LOW)
    grad_up = (grad_act * gate_silu).astype(LOW)
    grad_normed_two = (dot(grad_gate, ffn_w[0], NT) + dot(grad_up, ffn_w[1], NT)).astype(LOW)
    grad_two_other = swap(grad_normed_two[tok_rows:], "hid", 1)
    ffn_part = dot(activation, ffn_w[2], NT).astype(LOW)
    ffn_other = swap(after(ffn_part[tok_rows:], grad_two_other), "hid", 1)
    grad_two = grad_normed_two[:tok_rows].astype(F32) + grad_two_other.astype(F32)
    block_out = (
        (hidden + (ffn_part[:tok_rows].astype(F32) + ffn_other.astype(F32))).astype(LOW)[None]
    )
    grad_norm_two, gain_grad_two = norm_backward(hidden, inv_two, norm_gains[1], grad_two)
    grad_hidden = cotangent[0].astype(F32) + grad_norm_two
    grad_hidden_low = grad_hidden.astype(LOW)

    grad_mixed_own = dot(out_w, grad_hidden_low, NT).astype(LOW)
    grad_mixed = jnp.zeros((head_cols, length), LOW)
    grad_mixed = put(grad_mixed, take(grad_mixed_own, at_heads, head_cols, 0), at_heads, 1)
    for mask in range(n_heads - 1, 0, -1):
        block = swap(take(grad_mixed_own, at_heads ^ mask, head_cols, 0), "heads", mask)
        grad_mixed = put(grad_mixed, block, at_heads ^ mask, 1)

    ffn_grads = []
    for left, right in ((ffn_in, grad_gate), (ffn_in, grad_up), (ffn_back, activation)):
        part = dot(after(left, grad_two_other), right, TN).astype(LOW)
        part = part.reshape(n_seq, n_heads, -1, hidden_cols)
        size = n_heads
        bit = 1
        part = part.reshape(n_seq, n_heads, -1, hidden_cols)
        while size > 1:
            pairs = part.reshape(n_seq, size // 2, 2, -1, hidden_cols)
            side = lax.rem(at_heads // bit, 2)
            mine = lax.dynamic_index_in_dim(pairs, side, 2, False)
            other = lax.dynamic_index_in_dim(pairs, 1 - side, 2, False)
            moved = swap(other, "heads", bit)
            part = (mine.astype(F32) + moved.astype(F32)).astype(LOW)
            size //= 2
            bit *= 2
        part = part.reshape(n_seq, -1, hidden_cols)
        ffn_grads.append(
            ring_scatter(
                lambda at, part=part: lax.dynamic_index_in_dim(part, at, 0, False).astype(F32), "seq"
            )
        )
    gu_grad = jnp.stack(ffn_grads[:2])
    down_grad = ffn_grads[2].T

    def to_owner(grad):
        cols = model_width // (n_seq * n_hid)
        lead = grad.shape[:-1]
        parts = grad.reshape(*lead, n_seq, n_hid, cols)
        axis = len(lead) + 1
        mine = lax.dynamic_index_in_dim(parts, at_hid, axis, False)
        if n_hid > 1:
            other = lax.dynamic_index_in_dim(parts, at_hid ^ 1, axis, False)
            mine = (mine.astype(F32) + swap(other, "hid", 1).astype(F32)).astype(LOW)
        return ring_scatter(
            lambda at: lax.dynamic_index_in_dim(mine, at, axis - 1, False).astype(F32), "seq"
        )

    out_part = dot(mixed_own, grad_hidden_low, NN).astype(LOW)
    size, bit = n_heads, 1
    while size > 1:
        pairs = out_part.reshape(size // 2, 2, head_cols, model_width)
        side = lax.rem(at_heads // bit, 2)
        mine = lax.dynamic_index_in_dim(pairs, side, 1, False)
        other = lax.dynamic_index_in_dim(pairs, 1 - side, 1, False)
        out_part = (mine.astype(F32) + swap(other, "heads", bit).astype(F32)).astype(LOW)
        size //= 2
        bit *= 2
    out_grad = to_owner(out_part.reshape(head_cols, model_width))

    grad_queries, grad_keys, grad_values = attention_backward(
        queries, keys_rot, values, grad_mixed, mixed, lse, query_segs, key_segs
    )
    first_grad = ((1.0 - BLEND) * grad_values).T[None]
    grad_projected = jnp.concatenate(
        [
            rotate(grad_queries * query_scale, cosine, sine_table, -1.0).astype(LOW),
            rotate(grad_keys, cosine, sine_table, -1.0).astype(LOW),
            (BLEND * grad_values).astype(LOW),
        ],
        axis=0,
    )

    def partial_of(mask):
        return dot(take(grad_projected, at_heads ^ mask, tok_rows, 1), in_w, TN)

    sums = {}
    for mask in range(n_heads - 1, 0, -2):
        moved = swap(partial_of(mask).astype(LOW), "heads", near)
        sums[mask ^ near] = partial_of(mask ^ near) + moved.astype(F32)
    for bit in far_bits:
        for mask in sorted(sums, reverse=True):
            if mask & bit:
                moved = swap(sums.pop(mask).astype(LOW), "heads", bit)
                sums[mask ^ bit] = sums[mask ^ bit] + moved.astype(F32)
    grad_one = sums[0]
    in_part = dot(grad_projected, group_rows, NN).astype(LOW)
    in_grad = jnp.swapaxes(to_owner(in_part.reshape(3, head_cols, model_width)), 1, 2)
    grad_norm_one, gain_grad_one = norm_backward(own_rows, inv_one, norm_gains[0], grad_one)
    input_grad = (grad_hidden + grad_norm_one)[None]

    in_mean, in_var, in_update, in_wsq, in_usq = matrix_step(
        heads_in, heads_in_mean, heads_in_var, in_grad, (1, 2)
    )
    out_mean, out_var, out_update, out_wsq, out_usq = matrix_step(
        heads_out, heads_out_mean, heads_out_var, out_grad, (0, 1)
    )
    gu_mean, gu_var, gu_update, gu_wsq, gu_usq = matrix_step(
        gate_up, gate_up_mean, gate_up_var, gu_grad, (1, 2)
    )
    dn_mean, dn_var, dn_update, dn_wsq, dn_usq = matrix_step(
        down_proj, down_mean, down_var, down_grad, (0, 1)
    )
    weight_local = jnp.concatenate(
        [in_wsq.reshape(-1), out_wsq.reshape(-1), gu_wsq.reshape(-1), dn_wsq.reshape(-1)]
    )
    update_local = jnp.concatenate(
        [in_usq.reshape(-1), out_usq.reshape(-1), gu_usq.reshape(-1), dn_usq.reshape(-1)]
    )
    blended_wide = values.astype(jnp.float32)
    value_local = jnp.stack(
        [jnp.sum(first_local * first_local), jnp.sum(blended_wide * blended_wide)]
    )
    packed = jnp.concatenate([gain_grad_one, gain_grad_two, weight_local, update_local, value_local])
    packed = jnp.pad(packed, (0, -packed.shape[0] % 128)).reshape(-1, 128)
    for axis in ("heads", "seq", "hid"):
        packed = total(packed, axis)
    packed = packed.reshape(-1)
    gain_grads = packed[: 2 * model_width].reshape(2, model_width)
    weight_tot, update_tot, value_tot = (
        packed[2 * model_width + begin : 2 * model_width + finish]
        for begin, finish in ((0, 7), (7, 14), (14, 16))
    )
    ratios = jnp.sqrt(weight_tot) / jnp.sqrt(update_tot + 1e-12)
    in_new = heads_in - MATRIX_RATE * ratios[0:3].reshape(3, 1, 1) * in_update
    out_new = heads_out - MATRIX_RATE * ratios[3] * out_update
    gu_new = gate_up - MATRIX_RATE * ratios[4:6].reshape(2, 1, 1) * gu_update
    dn_new = down_proj - MATRIX_RATE * ratios[6] * dn_update
    gmean_new, gvar_new, gain_dir = adam_moments(gain_mean, gain_var, gain_grads)
    gains_new = norm_gains - GAIN_RATE * gain_dir
    entries = float(
        length * head_cols * lax.axis_size("seq") * lax.axis_size("heads") * lax.axis_size("hid")
    )
    norms = jnp.concatenate([jnp.sqrt(weight_tot), jnp.sqrt(update_tot)])
    value_norms = jnp.sqrt(value_tot / entries)
    return (
        block_out,
        input_grad,
        first_grad,
        gains_new,
        gmean_new,
        gvar_new,
        in_new,
        in_mean,
        in_var,
        out_new,
        out_mean,
        out_var,
        gu_new,
        gu_mean,
        gu_var,
        dn_new,
        dn_mean,
        dn_var,
        norms,
        value_norms,
    )


def solution(mesh):
    placed = (
        P(("seq", "hid"), "heads", None),
        P(("seq", "hid"), None, "heads"),
        P(("seq", "hid"), "heads", None),
        P(("seq", "hid"), None),
        P(("seq", "hid"), None),
        P(("seq", "hid"), None),
        P(),
        P(),
        P(),
        P(None, ("seq", "hid"), "heads"),
        P(None, ("seq", "hid"), "heads"),
        P(None, ("seq", "hid"), "heads"),
        P("heads", ("seq", "hid")),
        P("heads", ("seq", "hid")),
        P("heads", ("seq", "hid")),
        P(None, ("seq", "heads"), "hid"),
        P(None, ("seq", "heads"), "hid"),
        P(None, ("seq", "heads"), "hid"),
        P("hid", ("seq", "heads")),
        P("hid", ("seq", "heads")),
        P("hid", ("seq", "heads")),
    )
    return jax.shard_map(
        per_device,
        mesh=mesh,
        in_specs=placed,
        out_specs=(
            P(("seq", "hid"), "heads", None),
            P(("seq", "hid"), "heads", None),
            P(("seq", "hid"), None, "heads"),
            P(),
            P(),
            P(),
            P(None, ("seq", "hid"), "heads"),
            P(None, ("seq", "hid"), "heads"),
            P(None, ("seq", "hid"), "heads"),
            P("heads", ("seq", "hid")),
            P("heads", ("seq", "hid")),
            P("heads", ("seq", "hid")),
            P(None, ("seq", "heads"), "hid"),
            P(None, ("seq", "heads"), "hid"),
            P(None, ("seq", "heads"), "hid"),
            P("hid", ("seq", "heads")),
            P("hid", ("seq", "heads")),
            P("hid", ("seq", "heads")),
            P(),
            P(),
        ),
        check_vma=False,
    )
```

time: 951 us -> 498 us (0.52)
  waiting for transfers between devices: 476 us -> 193 us
  matrix products: 198 us -> 73.4 us
  other arithmetic: 122 us -> 47 us
  blocking collectives: 71.9 us -> 0 us
  starting transfers between devices: 0.81 us -> 46.2 us
  Pallas kernels: 0 us -> 36.5 us
  local copies, waits for them, and re-layouts: 58 us -> 90.5 us
  between operations: 19.1 us -> 3.99 us
    reduce_scatter x5 -> x0, waiting for transfers between devices: 194 us -> none  [the longest x1 81.5 us: per_device(): lax.psum_scatter(grad_down_w, ('seq', 'heads'), scatter_dimension=1, tile...]
    ppermute x0 -> x72, waiting for transfers between devices: none -> 193 us  [the longest x51 121 us: swap(): lax.ppermute(value, axis, [(i, i ^ mask) for i in range(lax.axis_size(axi...]
    all_gather x7 -> x0, waiting for transfers between devices: 165 us -> none  [the longest x1 43.2 us: per_device(): lax.all_gather(down_proj.astype(jnp.bfloat16), ('seq', 'heads'), axis=1,...]
    dot_general x36 -> x18, matrix products: 198 us -> 73.4 us  [dot(): lax.dot_general(left, right, (dims, ((), ())), preferred_element_type=F32)]
    unnamed x18 -> x0, waiting for transfers between devices: 117 us -> none
    ppermute x0 -> x72, starting transfers between devices: none -> 46.2 us  [the longest x51 37.7 us: swap(): lax.ppermute(value, axis, [(i, i ^ mask) for i in range(lax.axis_size(axi...]
    psum x1 -> x0, blocking collectives: 39.9 us -> none  [per_device(): lax.psum((gain_local, weight_local, update_local, value_local), ('seq', '...]
    pallas_call x0 -> x2, Pallas kernels: none -> 36.5 us  [the longest x1 23.3 us: attention_backward(): pl.pallas_call(functools.partial(attend_back_kernel, min(BLOCK, length)),...]
  transfers between devices with their start and end apart: 15 -> 72, of which waited for: 14 -> 31; matrix products, arithmetic and copies ran while one was open for 28% -> 31% of each run, Pallas kernels for 0% -> 7%
where the time goes in v1:
time: 498 us; the launch traced here: 491 us
  waiting for transfers between devices  193 us (39%)
  local copies, waits for them, and re-layouts  90.5 us (18%)
  matrix products  73.4 us (15%)
  other arithmetic  47 us (9%)
  starting transfers between devices  46.2 us (9%)
  Pallas kernels  36.5 us (7%)
    ppermute x51, waiting for transfers between devices, swap(): lax.ppermute(value, axis, [(i, i ^ mask) for i in range(lax.axis_size(axi...  121 us
    dot_general x18, matrix products, dot(): lax.dot_general(left, right, (dims, ((), ())), preferred_element_type=F32)  73.4 us
    ppermute x21, waiting for transfers between devices, ring(): return lax.ppermute(value, axis, [(i, (i + 1) % size) for i in range(size)])  72.5 us
    ppermute x51, starting transfers between devices, swap(): lax.ppermute(value, axis, [(i, i ^ mask) for i in range(lax.axis_size(axi...  37.7 us
    dynamic_update_slice x36, local copies, waits for them, and re-layouts, put(): lax.dynamic_update_slice_in_dim(buffer, value, index * value.shape[axis],...  29.7 us
    unnamed x161, local copies, waits for them, and re-layouts  26.9 us
    pallas_call x1, Pallas kernels, attention_backward(): pl.pallas_call(functools.partial(attend_back_kernel, min(BLOCK, length)),...  23.3 us
    pallas_call x1, Pallas kernels, attention_forward(): pl.pallas_call(functools.partial(attend_kernel, min(BLOCK, length)), grid...  13.2 us
  transfers between devices with their start and end apart: 72, of which 31 were waited for; matrix products, arithmetic and copies ran while one was open for 31% of the time, Pallas kernels for 7%

profile of v1, /device:TPU:0, one launch (start us, length us, event | category | flops | bytes accessed | tf_op | source)
XLA Modules:
  0.0 490.7 jit_solution(16091872631035716077)
XLA Ops:
  14.7 18.6 %collective-permute-done = bf16[256,128]{1,0:T(8,128)(2,1)S(1)} collective-permute-done((bf16[256,128]{1,0:T(8,128)(2,1)S(1)}, bf16[256,128]{1,0:T(8,128)(2,1)S(1)}, u32[]{:S(2)}, u32[]{:S(2)}) %collective-permute-start) | collective-permute-done | bytes 65568 | tf_op jit(solution)/shard_map/ppermute | solution.py:262
  37.9 7.7 %collective-permute-done.2 = bf16[5,256,128]{2,1,0:T(8,128)(2,1)} collective-permute-done((bf16[5,256,128]{2,1,0:T(8,128)(2,1)}, bf16[5,256,128]{2,1,0:T(8,128)(2,1)}, u32[]{:S(2)}, u32[]{:S(2)}) %collective-permute-start.2) | collective-permute-done | bytes 327712 | tf_op jit(solution)/shard_map/ppermute | solution.py:267
  72.5 5.8 %collective-permute-done.7 = bf16[5,256,128]{2,1,0:T(8,128)(2,1)S(1)} collective-permute-done((bf16[5,256,128]{2,1,0:T(8,128)(2,1)S(1)}, bf16[5,256,128]{2,1,0:T(8,128)(2,1)S(1)}, u32[]{:S(2)}, u32[]{:S(2)}) %collective-permute-start.7) | collective-permute-done | bytes 327712 | tf_op jit(solution)/shard_map/ppermute | solution.py:262
  81.2 5.5 %collective-permute-done.19 = bf16[3,64,1408]{2,1,0:T(8,128)(2,1)} collective-permute-done((bf16[3,64,1408]{2,1,0:T(8,128)(2,1)S(1)}, bf16[3,64,1408]{2,1,0:T(8,128)(2,1)}, u32[]{:S(2)}, u32[]{:S(2)}) %collective-permute-start.19) | collective-permute-done | bytes 540704 | tf_op jit(solution)/shard_map/ppermute | solution.py:267
  97.7 13.2 %shard_map.356 = (bf16[256,2048]{1,0:T(8,128)(2,1)S(1)}, f32[4,1,2048]{2,1,0:T(1,128)S(1)}) custom-call(bf16[256,2048]{1,0:T(8,128)(2,1)S(1)} %bitcast.251, bf16[256,2048]{1,0:T(8,128)(2,1)S(1)} %bitcast.253, bf16[256,2048]{1,0:T(8,128)(2,1)S(1)} %get-tuple-element.114.v_ref, s32[1,2048]{1,0:T(1,128)S(1)} %copy-done.4, s32[2048,1]{1,0:T(8,128)S(1)} %copy.52.kseg_ref, ...), custom_call_target="tpu_custom_call" | custom-call | flops 8589934592 | bytes 4194304 | tf_op jit(solution)/shard_map/pallas_call | solution.py:127
  121.0 4.6 collective-permute-done.12
  135.7 6.9 %collective-permute-done.27 = bf16[3,64,1408]{2,1,0:T(8,128)(2,1)S(1)} collective-permute-done((bf16[3,64,1408]{2,1,0:T(8,128)(2,1)}, bf16[3,64,1408]{2,1,0:T(8,128)(2,1)S(1)}, u32[]{:S(2)}, u32[]{:S(2)}) %collective-permute-start.27) | collective-permute-done | bytes 540704 | tf_op jit(solution)/shard_map/ppermute | solution.py:267
  146.6 9.9 %collective-permute-done.28 = bf16[3,64,1408]{2,1,0:T(8,128)(2,1)S(1)} collective-permute-done((bf16[3,64,1408]{2,1,0:T(8,128)(2,1)S(1)}, bf16[3,64,1408]{2,1,0:T(8,128)(2,1)S(1)}, u32[]{:S(2)}, u32[]{:S(2)}) %collective-permute-start.28) | collective-permute-done | bytes 540704 | tf_op jit(solution)/shard_map/ppermute | solution.py:262
  158.5 8.6 %collective-permute-done.15 = bf16[512,1024]{1,0:T(8,128)(2,1)S(1)} collective-permute-done((bf16[512,1024]{1,0:T(8,128)(2,1)S(1)}, bf16[512,1024]{1,0:T(8,128)(2,1)S(1)}, u32[]{:S(2)}, u32[]{:S(2)}) %collective-permute-start.15) | collective-permute-done | bytes 1048608 | tf_op jit(solution)/shard_map/ppermute | solution.py:262
  167.1 6.5 %fusion.7 = f32[1024,1408]{1,0:T(8,128)} fusion(bf16[3,1024,1408]{2,1,0:T(8,128)(2,1)S(1)} %constant_dynamic-update-slice_fusion.3, bf16[512,1024]{1,0:T(8,128)(2,1)S(1)} %collective-permute-done.15, bf16[512,1024]{1,0:T(8,128)(2,1)S(1)} %multiply_convert_fusion.3), kind=kOutput, calls=%fused_computation.28 | convolution fusion | flops 2956984320 | bytes 10747904 | tf_op jit(solution)/shard_map/dot_general | solution.py:36
  173.6 6.1 %fusion.8 = f32[1024,1408]{1,0:T(8,128)} fusion(bf16[3,1024,1408]{2,1,0:T(8,128)(2,1)S(1)} %constant_dynamic-update-slice_fusion.3, bf16[512,1024]{1,0:T(8,128)(2,1)S(1)} %collective-permute-done.31, bf16[512,1024]{1,0:T(8,128)(2,1)S(1)} %bitcast.260), kind=kOutput, calls=%fused_computation.29 | convolution fusion | flops 2956984320 | bytes 10747904 | tf_op jit(solution)/shard_map/dot_general | solution.py:36
  179.7 11.0 %multiply_convert_fusion.1 = (bf16[1024,1408]{1,0:T(8,128)(2,1)}, bf16[1024,1408]{1,0:T(8,128)(2,1)S(1)}, bf16[1024,1408]{1,0:T(8,128)(2,1)}) fusion(f32[1024,1408]{1,0:T(8,128)} %fusion.8, f32[1024,1408]{1,0:T(8,128)} %fusion.7, bf16[3,1024,1408]{2,1,0:T(8,128)(2,1)S(1)} %constant_dynamic-update-slice_fusion.3, ...), kind=kOutput, calls=%fused_computation.1 | convolution fusion | flops 2978611200 | bytes 25165824 | tf_op jit(solution)/shard_map/dot_general | solution.py:36
  204.7 16.8 %collective-permute-done.32 = bf16[512,1024]{1,0:T(8,128)(2,1)S(1)} collective-permute-done((bf16[512,1024]{1,0:T(8,128)(2,1)S(1)}, bf16[512,1024]{1,0:T(8,128)(2,1)S(1)}, u32[]{:S(2)}, u32[]{:S(2)}) %collective-permute-start.32) | collective-permute-done | bytes 1048608 | tf_op jit(solution)/shard_map/ppermute | solution.py:262
  223.4 3.9 convolution_convert_fusion
  272.2 23.3 %shard_map.357 = (f32[256,2048]{1,0:T(8,128)S(1)}, f32[256,2048]{1,0:T(8,128)S(1)}, f32[256,2048]{1,0:T(8,128)S(1)}) custom-call(bf16[256,2048]{1,0:T(8,128)(2,1)S(1)} %bitcast.252, bf16[256,2048]{1,0:T(8,128)(2,1)S(1)} %bitcast.254, bf16[256,2048]{1,0:T(8,128)(2,1)S(1)} %get-tuple-element.114.v_ref, ...), custom_call_target="tpu_custom_call" | custom-call | flops 21474836480 | bytes 11534336 | tf_op jit(solution)/shard_map/pallas_call | solution.py:235
  300.8 6.6 %convolution_convert_fusion.4 = bf16[768,1024]{1,0:T(8,128)(2,1)} fusion(bf16[2048,1024]{1,0:T(8,128)(2,1)S(1)} %copy-done.19, bf16[256,2048]{1,0:T(8,128)(2,1)S(1)} %get-tuple-element.142, bf16[256,2048]{1,0:T(8,128)(2,1)S(1)} %bitcast.265, bf16[256,2048]{1,0:T(8,128)(2,1)S(1)} %bitcast.263), kind=kOutput, calls=%fused_computation.68 | convolution fusion | flops 3231449088 | bytes 8912896 | tf_op jit(solution)/shard_map/dot_general | solution.py:36
  315.8 4.4 constant_dynamic-slice_fusion.7
  320.2 4.6 copy.55
  334.6 10.3 %collective-permute-done.40 = bf16[3,256,4,128]{1,3,0,2:T(8,128)(2,1)S(1)} collective-permute-done((bf16[3,256,4,128]{1,3,0,2:T(8,128)(2,1)}, bf16[3,256,4,128]{1,3,0,2:T(8,128)(2,1)S(1)}, u32[]{:S(2)}, u32[]{:S(2)}) %collective-permute-start.40) | collective-permute-done | bytes 786464 | tf_op jit(solution)/shard_map/ppermute | solution.py:262
  351.9 14.4 %collective-permute-done.51 = bf16[4,1,64,1408]{3,2,1,0:T(8,128)(2,1)S(1)} collective-permute-done((bf16[4,1,64,1408]{3,2,1,0:T(8,128)(2,1)S(1)}, bf16[4,1,64,1408]{3,2,1,0:T(8,128)(2,1)S(1)}, u32[]{:S(2)}, u32[]{:S(2)}) %collective-permute-start.51) | collective-permute-done | bytes 720928 | tf_op jit(solution)/shard_map/ppermute | solution.py:262
  366.9 14.8 %collective-permute-done.56 = bf16[4,1,64,1408]{3,2,1,0:T(8,128)(2,1)S(1)} collective-permute-done((bf16[4,1,64,1408]{3,2,1,0:T(8,128)(2,1)S(1)}, bf16[4,1,64,1408]{3,2,1,0:T(8,128)(2,1)S(1)}, u32[]{:S(2)}, u32[]{:S(2)}) %collective-permute-start.56) | collective-permute-done | bytes 720928 | tf_op jit(solution)/shard_map/ppermute | solution.py:262
  382.9 7.3 %collective-permute-done.62 = bf16[64,1408]{1,0:T(8,128)(2,1)S(1)} collective-permute-done((bf16[64,1408]{1,0:T(8,128)(2,1)S(1)}, bf16[64,1408]{1,0:T(8,128)(2,1)S(1)}, u32[]{:S(2)}, u32[]{:S(2)}) %collective-permute-start.62) | collective-permute-done | bytes 180256 | tf_op jit(solution)/shard_map/ppermute | solution.py:267
  393.7 4.4 collective-permute-done.57
  399.3 3.9 collective-permute-done.42
  403.3 4.1 collective-permute-done.63
  414.8 5.4 %collective-permute-done.43 = bf16[3,256,128]{1,2,0:T(8,128)(2,1)S(1)} collective-permute-done((bf16[3,256,128]{1,2,0:T(8,128)(2,1)S(1)}, bf16[3,256,128]{1,2,0:T(8,128)(2,1)S(1)}, u32[]{:S(2)}, u32[]{:S(2)}) %collective-permute-start.43) | collective-permute-done | bytes 196640 | tf_op jit(solution)/shard_map/ppermute | solution.py:267
  422.0 3.9 collective-permute-done.54
  427.4 4.8 collective-permute-done.46
  432.5 6.0 %collective-permute-done.47 = bf16[256,128]{0,1:T(8,128)(2,1)S(1)} collective-permute-done((bf16[256,128]{0,1:T(8,128)(2,1)S(1)}, bf16[256,128]{0,1:T(8,128)(2,1)S(1)}, u32[]{:S(2)}, u32[]{:S(2)}) %collective-permute-start.47) | collective-permute-done | bytes 65568 | tf_op jit(solution)/shard_map/ppermute | solution.py:267
  446.8 4.2 collective-permute-done.49
  455.8 4.8 concatenate.30
  470.3 4.2 collective-permute-start.70
  (437 shorter events, 230.2 us)
Async XLA Ops:
  5.6 56.6 %collective-permute-start.8 = (bf16[512,1024]{1,0:T(8,128)(2,1)}, bf16[512,1024]{1,0:T(8,128)(2,1)}, u32[]{:S(2)}, u32[]{:S(2)}) collective-permute-start(bf16[512,1024]{1,0:T(8,128)(2,1)} %get-tuple-element.125), channel_id=1, source_target_pairs={{0,4},{2,6},{4,0},{6,2},{1,5},{3,7},{5,1},{7,3},{8,12},{10,14},{12... | collective-permute-start | bytes 3145736 | tf_op jit(solution)/shard_map/ppermute | solution.py:262
  8.6 55.9 %collective-permute-start.9 = (bf16[512,1024]{1,0:T(8,128)(2,1)}, bf16[512,1024]{1,0:T(8,128)(2,1)}, u32[]{:S(2)}, u32[]{:S(2)}) collective-permute-start(bf16[512,1024]{1,0:T(8,128)(2,1)} %get-tuple-element.125), channel_id=1, source_target_pairs={{0,2},{2,0},{4,6},{6,4},{1,3},{3,1},{5,7},{7,5},{8,10},{10,8},{12,... | collective-permute-start | bytes 3145736 | tf_op jit(solution)/shard_map/ppermute | solution.py:262
  9.2 24.1 %collective-permute-start = (bf16[256,128]{1,0:T(8,128)(2,1)S(1)}, bf16[256,128]{1,0:T(8,128)(2,1)S(1)}, u32[]{:S(2)}, u32[]{:S(2)}) collective-permute-start(bf16[256,128]{1,0:T(8,128)(2,1)S(1)} %get-tuple-element.163), channel_id=1, source_target_pairs={{0,4},{2,6},{4,0},{6,2},{1,5},{3,7},{5,1},{7,3},{8,12},{10,14},{12... | collective-permute-start | bytes 196616 | tf_op jit(solution)/shard_map/ppermute | solution.py:262
  36.3 17.0 %collective-permute-start.1 = (bf16[5,256,128]{2,1,0:T(8,128)(2,1)}, bf16[5,256,128]{2,1,0:T(8,128)(2,1)}, u32[]{:S(2)}, u32[]{:S(2)}) collective-permute-start(bf16[5,256,128]{2,1,0:T(8,128)(2,1)} %get-tuple-element.160), channel_id=1, source_target_pairs={{0,1},{1,0},{2,3},{3,2},{4,5},{5,4},{6,7},{7,6},{8,9},{9,8},{10,11... | collective-permute-start | bytes 983048 | tf_op jit(solution)/shard_map/ppermute | solution.py:262
  62.2 26.9 %collective-permute-start.10 = (bf16[512,1024]{1,0:T(8,128)(2,1)}, bf16[512,1024]{1,0:T(8,128)(2,1)S(1)}, u32[]{:S(2)}, u32[]{:S(2)}) collective-permute-start(bf16[512,1024]{1,0:T(8,128)(2,1)} %collective-permute-done.8), channel_id=1, source_target_pairs={{0,2},{2,0},{4,6},{6,4},{1,3},{3,1},{5,7},{7,5},{8,10},{10,8},{12,... | collective-permute-start | bytes 3145736 | tf_op jit(solution)/shard_map/ppermute | solution.py:262
  66.8 20.5 %collective-permute-start.16 = (bf16[3,64,1408]{2,1,0:T(8,128)(2,1)S(1)}, bf16[3,64,1408]{2,1,0:T(8,128)(2,1)}, u32[]{:S(2)}, u32[]{:S(2)}) collective-permute-start(bf16[3,64,1408]{2,1,0:T(8,128)(2,1)S(1)} %pad_maximum_fusion.7), channel_id=1, source_target_pairs={{0,4},{2,6},{4,0},{6,2},{1,5},{3,7},{5,1},{7,3},{8,12},{10,14},{12... | collective-permute-start | bytes 1622024 | tf_op jit(solution)/shard_map/ppermute | solution.py:262
  68.2 20.2 %collective-permute-start.17 = (bf16[3,64,1408]{2,1,0:T(8,128)(2,1)S(1)}, bf16[3,64,1408]{2,1,0:T(8,128)(2,1)S(1)}, u32[]{:S(2)}, u32[]{:S(2)}) collective-permute-start(bf16[3,64,1408]{2,1,0:T(8,128)(2,1)S(1)} %pad_maximum_fusion.7), channel_id=1, source_target_pairs={{0,2},{2,0},{4,6},{6,4},{1,3},{3,1},{5,7},{7,5},{8,10},{10,8},{12,... | collective-permute-start | bytes 1622024 | tf_op jit(solution)/shard_map/ppermute | solution.py:262
  78.7 47.5 %collective-permute-start.14 = (bf16[2,256,1024]{2,1,0:T(8,128)(2,1)S(1)}, bf16[2,256,1024]{2,1,0:T(8,128)(2,1)}, u32[]{:S(2)}, u32[]{:S(2)}) collective-permute-start(bf16[2,256,1024]{2,1,0:T(8,128)(2,1)S(1)} %slice.182), channel_id=1, source_target_pairs={{0,2},{2,0},{4,6},{6,4},{1,3},{3,1},{5,7},{7,5},{8,10},{10,8},{12,... | collective-permute-start | bytes 3145736 | tf_op jit(solution)/shard_map/ppermute | solution.py:262
  86.7 27.7 %collective-permute-start.20 = (bf16[3,64,1408]{2,1,0:T(8,128)(2,1)}, bf16[3,64,1408]{2,1,0:T(8,128)(2,1)}, u32[]{:S(2)}, u32[]{:S(2)}) collective-permute-start(bf16[3,64,1408]{2,1,0:T(8,128)(2,1)} %collective-permute-done.19), channel_id=1, source_target_pairs={{0,4},{2,6},{4,0},{6,2},{1,5},{3,7},{5,1},{7,3},{8,12},{10,14},{12... | collective-permute-start | bytes 1622024 | tf_op jit(solution)/shard_map/ppermute | solution.py:262
  87.3 29.1 %collective-permute-start.21 = (bf16[3,64,1408]{2,1,0:T(8,128)(2,1)}, bf16[3,64,1408]{2,1,0:T(8,128)(2,1)}, u32[]{:S(2)}, u32[]{:S(2)}) collective-permute-start(bf16[3,64,1408]{2,1,0:T(8,128)(2,1)} %collective-permute-done.19), channel_id=1, source_target_pairs={{0,2},{2,0},{4,6},{6,4},{1,3},{3,1},{5,7},{7,5},{8,10},{10,8},{12,... | collective-permute-start | bytes 1622024 | tf_op jit(solution)/shard_map/ppermute | solution.py:262
  88.4 22.6 %collective-permute-start.18 = (bf16[3,64,1408]{2,1,0:T(8,128)(2,1)}, bf16[3,64,1408]{2,1,0:T(8,128)(2,1)}, u32[]{:S(2)}, u32[]{:S(2)}) collective-permute-start(bf16[3,64,1408]{2,1,0:T(8,128)(2,1)} %collective-permute-done.16), channel_id=1, source_target_pairs={{0,2},{2,0},{4,6},{6,4},{1,3},{3,1},{5,7},{7,5},{8,10},{10,8},{12,... | collective-permute-start | bytes 1622024 | tf_op jit(solution)/shard_map/ppermute | solution.py:262
  89.1 28.5 %collective-permute-start.23 = (bf16[3,64,1408]{2,1,0:T(8,128)(2,1)}, bf16[3,64,1408]{2,1,0:T(8,128)(2,1)}, u32[]{:S(2)}, u32[]{:S(2)}) collective-permute-start(bf16[3,64,1408]{2,1,0:T(8,128)(2,1)} %collective-permute-done.19), channel_id=1, source_target_pairs={{0,8},{8,16},{16,24},{24,0},{1,9},{9,17},{17,25},{25,1},{2,10},{10... | collective-permute-start | bytes 1622024 | tf_op jit(solution)/shard_map/ppermute | solution.py:267
  117.6 56.0 %collective-permute-start.31 = (bf16[512,1024]{1,0:T(8,128)(2,1)S(1)}, bf16[512,1024]{1,0:T(8,128)(2,1)S(1)}, u32[]{:S(2)}, u32[]{:S(2)}) collective-permute-start(bf16[512,1024]{1,0:T(8,128)(2,1)S(1)} %bitcast.259), channel_id=1, source_target_pairs={{0,1},{1,0},{2,3},{3,2},{4,5},{5,4},{6,7},{7,6},{8,9},{9,8},{10,11... | collective-permute-start | bytes 3145736 | tf_op jit(solution)/shard_map/ppermute | solution.py:262
  119.5 25.1 %collective-permute-start.24 = (bf16[3,64,1408]{2,1,0:T(8,128)(2,1)}, bf16[3,64,1408]{2,1,0:T(8,128)(2,1)S(1)}, u32[]{:S(2)}, u32[]{:S(2)}) collective-permute-start(bf16[3,64,1408]{2,1,0:T(8,128)(2,1)} %collective-permute-done.23), channel_id=1, source_target_pairs={{0,4},{2,6},{4,0},{6,2},{1,5},{3,7},{5,1},{7,3},{8,12},{10,14},{12... | collective-permute-start | bytes 1622024 | tf_op jit(solution)/shard_map/ppermute | solution.py:262
  125.6 20.3 %collective-permute-start.25 = (bf16[3,64,1408]{2,1,0:T(8,128)(2,1)}, bf16[3,64,1408]{2,1,0:T(8,128)(2,1)S(1)}, u32[]{:S(2)}, u32[]{:S(2)}) collective-permute-start(bf16[3,64,1408]{2,1,0:T(8,128)(2,1)} %collective-permute-done.23), channel_id=1, source_target_pairs={{0,2},{2,0},{4,6},{6,4},{1,3},{3,1},{5,7},{7,5},{8,10},{10,8},{12,... | collective-permute-start | bytes 1622024 | tf_op jit(solution)/shard_map/ppermute | solution.py:262
  125.6 17.6 %collective-permute-start.22 = (bf16[3,64,1408]{2,1,0:T(8,128)(2,1)}, bf16[3,64,1408]{2,1,0:T(8,128)(2,1)S(1)}, u32[]{:S(2)}, u32[]{:S(2)}) collective-permute-start(bf16[3,64,1408]{2,1,0:T(8,128)(2,1)} %collective-permute-done.20), channel_id=1, source_target_pairs={{0,2},{2,0},{4,6},{6,4},{1,3},{3,1},{5,7},{7,5},{8,10},{10,8},{12,... | collective-permute-start | bytes 1622024 | tf_op jit(solution)/shard_map/ppermute | solution.py:262
  142.7 24.4 %collective-permute-start.15 = (bf16[512,1024]{1,0:T(8,128)(2,1)S(1)}, bf16[512,1024]{1,0:T(8,128)(2,1)S(1)}, u32[]{:S(2)}, u32[]{:S(2)}) collective-permute-start(bf16[512,1024]{1,0:T(8,128)(2,1)S(1)} %multiply_convert_fusion.3), channel_id=1, source_target_pairs={{0,1},{1,0},{2,3},{3,2},{4,5},{5,4},{6,7},{7,6},{8,9},{9,8},{10,11... | collective-permute-start | bytes 3145736 | tf_op jit(solution)/shard_map/ppermute | solution.py:262
  198.0 23.5 %collective-permute-start.32 = (bf16[512,1024]{1,0:T(8,128)(2,1)S(1)}, bf16[512,1024]{1,0:T(8,128)(2,1)S(1)}, u32[]{:S(2)}, u32[]{:S(2)}) collective-permute-start(bf16[512,1024]{1,0:T(8,128)(2,1)S(1)} %slice.191), channel_id=1, source_target_pairs={{0,1},{1,0},{2,3},{3,2},{4,5},{5,4},{6,7},{7,6},{8,9},{9,8},{10,11... | collective-permute-start | bytes 3145736 | tf_op jit(solution)/shard_map/ppermute | solution.py:262
  221.5 22.6 %collective-permute-start.33 = (bf16[512,1024]{1,0:T(8,128)(2,1)S(1)}, bf16[512,1024]{1,0:T(8,128)(2,1)S(1)}, u32[]{:S(2)}, u32[]{:S(2)}) collective-permute-start(bf16[512,1024]{1,0:T(8,128)(2,1)S(1)} %slice.190), channel_id=1, source_target_pairs={{0,1},{1,0},{2,3},{3,2},{4,5},{5,4},{6,7},{7,6},{8,9},{9,8},{10,11... | collective-permute-start | bytes 3145736 | tf_op jit(solution)/shard_map/ppermute | solution.py:262
  229.3 97.5 %collective-permute-start.60 = (bf16[4,2,64,1408]{3,2,1,0:T(8,128)(2,1)}, bf16[4,2,64,1408]{3,2,1,0:T(8,128)(2,1)}, u32[]{:S(2)}, u32[]{:S(2)}) collective-permute-start(bf16[4,2,64,1408]{3,2,1,0:T(8,128)(2,1)} %dynamic-slice_bitcast_fusion), channel_id=1, source_target_pairs={{0,2},{2,0},{4,6},{6,4},{1,3},{3,1},{5,7},{7,5},{8,10},{10,8},{12,... | collective-permute-start | bytes 4325384 | tf_op jit(solution)/shard_map/ppermute | solution.py:262
  235.3 94.0 %collective-permute-start.50 = (bf16[4,2,64,1408]{3,2,1,0:T(8,128)(2,1)}, bf16[4,2,64,1408]{3,2,1,0:T(8,128)(2,1)}, u32[]{:S(2)}, u32[]{:S(2)}) collective-permute-start(bf16[4,2,64,1408]{3,2,1,0:T(8,128)(2,1)} %dynamic-slice_bitcast_fusion.2), channel_id=1, source_target_pairs={{0,2},{2,0},{4,6},{6,4},{1,3},{3,1},{5,7},{7,5},{8,10},{10,8},{12,... | collective-permute-start | bytes 4325384 | tf_op jit(solution)/shard_map/ppermute | solution.py:262
  261.0 70.8 %collective-permute-start.55 = (bf16[4,2,64,1408]{3,2,1,0:T(8,128)(2,1)}, bf16[4,2,64,1408]{3,2,1,0:T(8,128)(2,1)}, u32[]{:S(2)}, u32[]{:S(2)}) collective-permute-start(bf16[4,2,64,1408]{3,2,1,0:T(8,128)(2,1)} %dynamic-slice_bitcast_fusion.1), channel_id=1, source_target_pairs={{0,2},{2,0},{4,6},{6,4},{1,3},{3,1},{5,7},{7,5},{8,10},{10,8},{12,... | collective-permute-start | bytes 4325384 | tf_op jit(solution)/shard_map/ppermute | solution.py:262
  266.3 78.8 %collective-permute-start.44 = (bf16[2,256,1024]{1,2,0:T(8,128)(2,1)}, bf16[2,256,1024]{1,2,0:T(8,128)(2,1)}, u32[]{:S(2)}, u32[]{:S(2)}) collective-permute-start(bf16[2,256,1024]{1,2,0:T(8,128)(2,1)} %bitcast.280), channel_id=1, source_target_pairs={{0,2},{2,0},{4,6},{6,4},{1,3},{3,1},{5,7},{7,5},{8,10},{10,8},{12,... | collective-permute-start | bytes 3145736 | tf_op jit(solution)/shard_map/ppermute | solution.py:262
  324.8 20.0 %collective-permute-start.40 = (bf16[3,256,4,128]{1,3,0,2:T(8,128)(2,1)}, bf16[3,256,4,128]{1,3,0,2:T(8,128)(2,1)S(1)}, u32[]{:S(2)}, u32[]{:S(2)}) collective-permute-start(bf16[3,256,4,128]{1,3,0,2:T(8,128)(2,1)} %bitcast.42), channel_id=1, source_target_pairs={{0,1},{1,0},{2,3},{3,2},{4,5},{5,4},{6,7},{7,6},{8,9},{9,8},{10,11... | collective-permute-start | bytes 2359304 | tf_op jit(solution)/shard_map/ppermute | solution.py:262
  326.8 125.6 %collective-permute-start.37 = (bf16[512,1024]{1,0:T(8,128)(2,1)}, bf16[512,1024]{1,0:T(8,128)(2,1)S(1)}, u32[]{:S(2)}, u32[]{:S(2)}) collective-permute-start(bf16[512,1024]{1,0:T(8,128)(2,1)} %convolution_convert_fusion.6), channel_id=1, source_target_pairs={{0,2},{2,0},{4,6},{6,4},{1,3},{3,1},{5,7},{7,5},{8,10},{10,8},{12,... | collective-permute-start | bytes 3145736 | tf_op jit(solution)/shard_map/ppermute | solution.py:262
  329.3 68.9 %collective-permute-start.38 = (bf16[512,1024]{1,0:T(8,128)(2,1)S(1)}, bf16[512,1024]{1,0:T(8,128)(2,1)S(1)}, u32[]{:S(2)}, u32[]{:S(2)}) collective-permute-start(bf16[512,1024]{1,0:T(8,128)(2,1)S(1)} %copy-done.70), channel_id=1, source_target_pairs={{0,2},{2,0},{4,6},{6,4},{1,3},{3,1},{5,7},{7,5},{8,10},{10,8},{12,... | collective-permute-start | bytes 3145736 | tf_op jit(solution)/shard_map/ppermute | solution.py:262
  331.8 19.1 %collective-permute-start.61 = (bf16[4,1,64,1408]{3,2,1,0:T(8,128)(2,1)S(1)}, bf16[4,1,64,1408]{3,2,1,0:T(8,128)(2,1)S(1)}, u32[]{:S(2)}, u32[]{:S(2)}) collective-permute-start(bf16[4,1,64,1408]{3,2,1,0:T(8,128)(2,1)S(1)} %constant_dynamic-slice_fusion), channel_id=1, source_target_pairs={{0,4},{2,6},{4,0},{6,2},{1,5},{3,7},{5,1},{7,3},{8,12},{10,14},{12... | collective-permute-start | bytes 2162696 | tf_op jit(solution)/shard_map/ppermute | solution.py:262
  344.8 21.4 %collective-permute-start.51 = (bf16[4,1,64,1408]{3,2,1,0:T(8,128)(2,1)S(1)}, bf16[4,1,64,1408]{3,2,1,0:T(8,128)(2,1)S(1)}, u32[]{:S(2)}, u32[]{:S(2)}) collective-permute-start(bf16[4,1,64,1408]{3,2,1,0:T(8,128)(2,1)S(1)} %constant_dynamic-slice_fusion.2), channel_id=1, source_target_pairs={{0,4},{2,6},{4,0},{6,2},{1,5},{3,7},{5,1},{7,3},{8,12},{10,14},{12... | collective-permute-start | bytes 2162696 | tf_op jit(solution)/shard_map/ppermute | solution.py:262
  345.1 36.6 %collective-permute-start.56 = (bf16[4,1,64,1408]{3,2,1,0:T(8,128)(2,1)S(1)}, bf16[4,1,64,1408]{3,2,1,0:T(8,128)(2,1)S(1)}, u32[]{:S(2)}, u32[]{:S(2)}) collective-permute-start(bf16[4,1,64,1408]{3,2,1,0:T(8,128)(2,1)S(1)} %constant_dynamic-slice_fusion.1), channel_id=1, source_target_pairs={{0,4},{2,6},{4,0},{6,2},{1,5},{3,7},{5,1},{7,3},{8,12},{10,14},{12... | collective-permute-start | bytes 2162696 | tf_op jit(solution)/shard_map/ppermute | solution.py:262
  350.8 63.6 %collective-permute-start.45 = (bf16[1,256,1024]{1,2,0:T(8,128)(2,1)S(1)}, bf16[1,256,1024]{1,2,0:T(8,128)(2,1)S(1)}, u32[]{:S(2)}, u32[]{:S(2)}) collective-permute-start(bf16[1,256,1024]{1,2,0:T(8,128)(2,1)S(1)} %constant_dynamic-slice_fusion.3), channel_id=1, source_target_pairs={{0,4},{2,6},{4,0},{6,2},{1,5},{3,7},{5,1},{7,3},{8,12},{10,14},{12... | collective-permute-start | bytes 1572872 | tf_op jit(solution)/shard_map/ppermute | solution.py:262
  407.4 45.0 %collective-permute-start.39 = (bf16[512,1024]{1,0:T(8,128)(2,1)S(1)}, bf16[512,1024]{1,0:T(8,128)(2,1)S(1)}, u32[]{:S(2)}, u32[]{:S(2)}) collective-permute-start(bf16[512,1024]{1,0:T(8,128)(2,1)S(1)} %add_convert_fusion.1), channel_id=1, source_target_pairs={{0,4},{2,6},{4,0},{6,2},{1,5},{3,7},{5,1},{7,3},{8,12},{10,14},{12... | collective-permute-start | bytes 3145736 | tf_op jit(solution)/shard_map/ppermute | solution.py:262
  414.4 30.5 %collective-permute-start.64 = (bf16[64,1408]{1,0:T(8,128)(2,1)S(1)}, bf16[64,1408]{1,0:T(8,128)(2,1)S(1)}, u32[]{:S(2)}, u32[]{:S(2)}) collective-permute-start(bf16[64,1408]{1,0:T(8,128)(2,1)S(1)} %fusion.48), channel_id=1, source_target_pairs={{0,8},{8,16},{16,24},{24,0},{1,9},{9,17},{17,25},{25,1},{2,10},{10... | collective-permute-start | bytes 540680 | tf_op jit(solution)/shard_map/ppermute | solution.py:267
  (115 other events, 1073.5 us)
